TPU v7x, 32 devices: a whole 2x2x4 slice. The times are simulated.
32 devices in a mesh: dp: 16 (over z, y, core), mp: 2 (over x).
Axes of the slice: x: 2, y: 2, z: 4, core: 2. Of those that a mesh axis runs over, the one named last changes fastest.
Arguments:
- tiles: bfloat16 [8192, 1152], P('dp'), may hold values from -6 to 6
- norm_gain: float32 [1152], replicated, may hold values from 0.1 to 1.9
- norm_bias: float32 [1152], replicated, may hold values from -3 to 3
- expand_weight: bfloat16 [1152, 4304], P(None, 'mp'), may hold values from -0.1875 to 0.1875
- reduce_weight: bfloat16 [4304, 1152], P('mp'), may hold values from -0.09375 to 0.09375
- projector: bfloat16 [1152, 8192], P(None, 'mp'), may hold values from -0.1875 to 0.1875
- projector_bias: float32 [8192], P('mp'), may hold values from -3 to 3
- tile_counts: int32 [16, 2], replicated, may hold values from 1 to 9, as said below
- tile_owner: int32 [16, 16], replicated, may hold values from 0 to 15, as said below
- tile_slot: int32 [16, 16], replicated, may hold values from 0 to 15, as said below
- segment_ids: int32 [16, 640], P('dp'), may hold values from 0 to 3, never falling along the last dimension, each value on 1 to 320 neighbouring positions
- text_embed: bfloat16 [10240, 8192], P('dp', 'mp'), may hold values from -6 to 6
- input_gain: float32 [8192], replicated, may hold values from 0.6 to 8
- q_weight: bfloat16 [8192, 4096], P('dp', 'mp'), may hold values from -0.044194174 to 0.044194174
- k_weight: bfloat16 [8192, 1024], P('dp', 'mp'), may hold values from -0.044194174 to 0.044194174
- v_weight: bfloat16 [8192, 1024], P('dp', 'mp'), may hold values from -0.0625 to 0.0625
- feature_grad: bfloat16 [8192, 1152], P('dp'), may hold values from -6 to 6
Outputs:
- context: bfloat16 [10240, 4096], P('dp', 'mp')
- expand_grad: float32 [1152, 4304], P('dp', 'mp')
- reduce_grad_t: float32 [1152, 4304], P('dp', 'mp')
Inputs may be any that keep to these rules, and one draw needn't show every extreme that they name: `tile_counts`: each index of dp has two images, together at most 16 tiles; some index has exactly 16, some image has 9. `tile_owner`: the tile slots of one index of dp name distinct owners; every owner is named by exactly 16 tile slots in all, at most one of each index. `tile_slot`: the tile slots that name one owner name distinct image slots.
All inputs are finite; a program needn't handle non-finite values.
Results may differ from a plain program's by a relative error of at most 0.011.
Values may be sent and summed in bfloat16 or wider, within the bound.
A program may use at most 256 MiB of HBM per device.

v0:
```python
import math

import jax
import jax.numpy as jnp
from jax import lax
from jax.sharding import PartitionSpec as P

D = 8192
HEAD = 128
TILE_ROWS = 32


def encoder_front(tiles, norm_gain, norm_bias, expand_weight):
    values = tiles.astype(jnp.float32)
    center = values - jnp.mean(values, axis=1, keepdims=True)
    variance = jnp.mean(center * center, axis=1, keepdims=True)
    normed = (center * lax.rsqrt(variance + 1e-06) * norm_gain + norm_bias).astype(jnp.bfloat16)
    pre_act = jnp.dot(normed, expand_weight, preferred_element_type=jnp.float32)
    hidden_units = jax.nn.gelu(pre_act, approximate=True).astype(jnp.bfloat16)
    return (normed, pre_act, hidden_units)


def gelu_slope(pre_act):
    factor = math.sqrt(2.0 / math.pi)
    inner = factor * (pre_act + 0.044715 * pre_act**3)
    tangent = jnp.tanh(inner)
    return 0.5 * (1.0 + tangent) + 0.5 * pre_act * (1.0 - tangent * tangent) * factor * (
        1.0 + 3.0 * 0.044715 * pre_act * pre_act
    )


def segment_positions(segments):
    count = segments.shape[0]
    index = jnp.arange(count, dtype=jnp.int32)
    same = segments[:, None] == segments[None, :]
    first = jnp.min(jnp.where(same, index[None, :], count), axis=1)
    return index - first


def rotate(values, positions):
    width = values.shape[-1]
    half = width // 2
    freq = 1000000.0 ** (-(jnp.arange(half, dtype=jnp.float32) * 2.0 / width))
    angle = positions.astype(jnp.float32)[:, None] * freq[None, :]
    cosine = jnp.concatenate([jnp.cos(angle), jnp.cos(angle)], axis=1)[:, None, :]
    sine = jnp.concatenate([jnp.sin(angle), jnp.sin(angle)], axis=1)[:, None, :]
    turned = jnp.concatenate([-values[..., half:], values[..., :half]], axis=-1)
    return values * cosine + turned * sine


def attend(queries, keys, values, segments):
    count = queries.shape[0]
    kv_heads = keys.shape[1]
    grouped = queries.reshape(count, kv_heads, queries.shape[1] // kv_heads, queries.shape[2])
    scores = jnp.einsum("qgrd,kgd->grqk", grouped, keys, preferred_element_type=jnp.float32) * (
        1.0 / math.sqrt(queries.shape[2])
    )
    index = jnp.arange(count, dtype=jnp.int32)
    allowed = (index[None, :] <= index[:, None]) & (segments[None, :] == segments[:, None])
    scores = jnp.where(allowed[None, None], scores, -1e30)
    top = jnp.max(scores, axis=-1, keepdims=True)
    weights = jnp.exp(scores - top)
    probs = (weights / jnp.sum(weights, axis=-1, keepdims=True)).astype(jnp.bfloat16)
    context = jnp.einsum("grqk,kgd->qgrd", probs, values, preferred_element_type=jnp.float32)
    return context.reshape(count, -1).astype(jnp.bfloat16)


def body(
    tiles,
    norm_gain,
    norm_bias,
    expand_weight,
    reduce_weight,
    projector,
    projector_bias,
    tile_counts,
    tile_owner,
    tile_slot,
    segment_ids,
    text_embed,
    input_gain,
    q_weight,
    k_weight,
    v_weight,
    feature_grad,
):
    group_size = lax.axis_size("dp")
    my_index = lax.axis_index("dp")
    slot_count = tile_owner.shape[1]
    tile_rows = TILE_ROWS
    enc_rows = tiles.shape[0]
    totals = jnp.sum(tile_counts, axis=1)
    slot_ids = jnp.arange(slot_count, dtype=jnp.int32)
    live_all = slot_ids[None, :] < totals[:, None]
    my_live = lax.dynamic_index_in_dim(live_all, my_index, 0, keepdims=False)
    my_owner = lax.dynamic_index_in_dim(tile_owner, my_index, 0, keepdims=False)
    normed, pre_act, hidden_units = encoder_front(tiles, norm_gain, norm_bias, expand_weight)
    summed = lax.psum(
        jnp.dot(hidden_units, reduce_weight, preferred_element_type=jnp.float32), "mp"
    )
    enc_out = (tiles.astype(jnp.float32) + summed).astype(jnp.bfloat16)
    outgoing = (
        (jnp.arange(group_size, dtype=jnp.int32)[:, None] == my_owner[None, :]) & my_live[None, :]
    ).astype(jnp.bfloat16)
    match = (tile_owner == my_index) & live_all
    filled = jnp.any(match, axis=1)
    slot_used = jnp.sum(jnp.where(match, tile_slot, 0), axis=1)
    placing = (filled[None, :] & (slot_used[None, :] == slot_ids[:, None])).astype(jnp.bfloat16)
    projected = (
        jnp.dot(enc_out, projector, preferred_element_type=jnp.float32) + projector_bias
    ).astype(jnp.bfloat16)
    flat_tiles = projected.reshape(slot_count, -1)
    outbound = (
        jnp.dot(outgoing, flat_tiles, preferred_element_type=jnp.float32)
        .astype(jnp.bfloat16)
        .reshape(group_size, tile_rows, -1)
    )
    inbound = lax.all_to_all(outbound, "dp", split_axis=0, concat_axis=0, tiled=True)
    images = (
        jnp.dot(placing, inbound.reshape(group_size, -1), preferred_element_type=jnp.float32)
        .astype(jnp.bfloat16)
        .reshape(enc_rows, -1)
    )
    is_image = jnp.repeat(jnp.sum(placing, axis=1) > 0, tile_rows)[:, None]
    stream = jnp.concatenate(
        [jnp.where(is_image, images, text_embed[:enc_rows]), text_embed[enc_rows:]], axis=0
    )
    mb_rows = stream.shape[0]
    full_weights = (
        lax.all_gather(q_weight, "dp", axis=0, tiled=True),
        lax.all_gather(k_weight, "dp", axis=0, tiled=True),
        lax.all_gather(v_weight, "dp", axis=0, tiled=True),
    )
    piece_values = lax.all_gather(stream, "mp", axis=1, tiled=True).astype(jnp.float32)
    scaled_piece = (piece_values * input_gain).astype(jnp.bfloat16)
    sums = jnp.sum(piece_values * piece_values, axis=1)
    products = tuple(
        (
            jnp.dot(scaled_piece, full_weights[number], preferred_element_type=jnp.float32)
            for number in range(3)
        )
    )
    q_raw, k_raw, v_raw, squares = products + (sums,)
    inverse = lax.rsqrt(squares / D + 1e-06)[:, None]
    segments = segment_ids[0]
    positions = segment_positions(segments)
    queries = rotate((q_raw * inverse).reshape(mb_rows, -1, HEAD), positions).astype(jnp.bfloat16)
    keys = rotate((k_raw * inverse).reshape(mb_rows, -1, HEAD), positions).astype(jnp.bfloat16)
    values = (v_raw * inverse).reshape(mb_rows, -1, HEAD).astype(jnp.bfloat16)
    context = attend(queries, keys, values, segments)
    live_rows = jnp.repeat(my_live, tile_rows)[:, None]
    cotangent = jnp.where(live_rows, feature_grad, jnp.zeros_like(feature_grad))
    hidden_grad = lax.dot_general(
        cotangent, reduce_weight, (((1,), (1,)), ((), ())), preferred_element_type=jnp.float32
    )
    act_grad = (hidden_grad * gelu_slope(pre_act)).astype(jnp.bfloat16)
    reduce_grad_t = lax.dot_general(
        cotangent, hidden_units, (((0,), (0,)), ((), ())), preferred_element_type=jnp.float32
    )
    expand_grad = lax.dot_general(
        normed, act_grad, (((0,), (0,)), ((), ())), preferred_element_type=jnp.float32
    )
    expand_grad, reduce_grad_t = (
        lax.psum_scatter(expand_grad, "dp", scatter_dimension=0, tiled=True),
        lax.psum_scatter(reduce_grad_t, "dp", scatter_dimension=0, tiled=True),
    )
    return (context, expand_grad, reduce_grad_t)


def solution(mesh):
    in_specs = (
        P("dp", None),
        P(),
        P(),
        P(None, "mp"),
        P("mp", None),
        P(None, "mp"),
        P("mp"),
        P(),
        P(),
        P(),
        P("dp", None),
        P("dp", "mp"),
        P(),
        P("dp", "mp"),
        P("dp", "mp"),
        P("dp", "mp"),
        P("dp", None),
    )
    out_specs = (P("dp", "mp"), P("dp", "mp"), P("dp", "mp"))
    return jax.shard_map(body, mesh=mesh, in_specs=in_specs, out_specs=out_specs, check_vma=False)
```

profile of v0, /device:TPU:0, one launch (start us, length us, event | category | flops | bytes accessed | tf_op | source)
XLA Modules:
  0.0 934.6 jit_solution(3400280103328425548)
XLA Ops:
  10.6 5.8 fusion.85
  18.6 5.0 fusion.87
  23.8 71.2 %all-reduce.4.cloned.1.call-done = f32[512,1152]{1,0:T(8,128)} async-done(((f32[512,1152]{1,0:T(8,128)}), f32[512,1152]{1,0:T(8,128)}) %all-reduce.4.cloned.1.call-update) | async-done | bytes 2359312 | tf_op jit(solution)/shard_map/psum | solution.py:98
  95.1 10.2 %add_convert_fusion = bf16[512,4096]{1,0:T(8,128)(2,1)} fusion(bf16[1152,4096]{1,0:T(8,128)(2,1)} %param.22, f32[4096]{0:T(1024)S(1)} %copy-done.7, f32[512,1152]{1,0:T(8,128)} %all-reduce.4.cloned.1.call-done, bf16[512,1152]{1,0:T(8,128)(2,1)S(1)} %copy-done), kind=kOutput, calls=%fused_computation.15 | convolution fusion | flops 4837801984 | bytes 17186816 | tf_op jit(solution)/shard_map/dot_general | solution.py:110
  105.3 4.8 reshape.120
  113.6 4.3 copy.56
  117.8 5.8 all-to-all-start
  124.3 77.0 %all-to-all-done = bf16[16,32,4096]{2,1,0:T(8,128)(2,1)} async-done(((bf16[16,32,4096]{2,1,0:T(8,128)(2,1)}), bf16[16,32,4096]{2,1,0:T(8,128)(2,1)}, u32[]{:S(2)}, u32[]{:S(2)}) %all-to-all-start) | async-done | bytes 4194336 | tf_op jit(solution)/shard_map/all_to_all | solution.py:118
  201.3 4.5 copy.57
  209.0 4.8 reshape.123
  213.8 3.9 slice_select_fusion
  222.7 14.5 %fusion.56 = f32[1152,2152]{1,0:T(8,128)} fusion(bf16[2152,1152]{1,0:T(8,128)(2,1)} %param.21, f32[512,2152]{0,1:T(8,128)} %copy-done.11, bf16[512,1152]{1,0:T(8,128)(2,1)S(1)} %copy-done.5, pred[512]{0:T(512)(128)(4,1)S(1)} %broadcast_in_dim.57, bf16[512,1152]{1,0:T(8,128)(2,1)S(1)} %copy-done, f32[1152]{0:T(1024)S(1)} %copy-done.8, ...), kind=kOutput, calls=%fused_computation.63 | convolution fusion | flops 5102268416 | bytes 21655040 | tf_op jit(solution)/shard_map/dot_general | solution.py:160
  237.8 10.9 %fusion.58 = f32[1152,2152]{1,0:T(8,128)} fusion(bf16[512,1152]{1,0:T(8,128)(2,1)S(1)} %copy-done.5, pred[512]{0:T(512)(128)(4,1)S(1)} %broadcast_in_dim.57, f32[512,2152]{0,1:T(8,128)} %copy-done.11), kind=kOutput, calls=%fused_computation.65 | convolution fusion | flops 2549108736 | bytes 15503872 | tf_op jit(solution)/shard_map/dot_general | solution.py:157
  252.2 112.1 %all-gather.5.cloned.1.call-done = bf16[640,8192]{1,0:T(8,128)(2,1)} async-done(((bf16[640,4096]{1,0:T(8,128)(2,1)}), bf16[640,8192]{1,0:T(8,128)(2,1)}) %all-gather.5.cloned.1.call-update) | async-done | bytes 10485776 | tf_op jit(solution)/shard_map/all_gather | solution.py:134
  364.3 6.1 fusion.2
  370.4 71.2 %all-gather.9.cloned.1.call-done = bf16[8192,512]{1,0:T(8,128)(2,1)} async-done(((bf16[512,512]{1,0:T(8,128)(2,1)}), bf16[8192,512]{1,0:T(8,128)(2,1)}) %all-gather.9.cloned.1.call-update) | async-done | bytes 8388624 | tf_op jit(solution)/shard_map/all_gather | solution.py:131
  441.6 16.3 %fusion.47 = f32[640,512]{0,1:T(8,128)S(1)} fusion(bf16[8192,512]{1,0:T(8,128)(2,1)} %all-gather.9.cloned.1.call-done, bf16[640,8192]{1,0:T(8,128)(2,1)} %all-gather.5.cloned.1.call-done, f32[8192]{0:T(1024)S(1)} %copy-done.6, f32[640]{0:T(1024)S(1)} %add_rsqrt_fusion), kind=kOutput, calls=%fused_computation.56 | convolution fusion | flops 5384765440 | bytes 20220416 | tf_op jit(solution)/shard_map/dot_general | solution.py:139
  460.1 57.0 %all-gather.7.cloned.1.call-done = bf16[8192,512]{1,0:T(8,128)(2,1)} async-done(((bf16[512,512]{1,0:T(8,128)(2,1)}), bf16[8192,512]{1,0:T(8,128)(2,1)}) %all-gather.7.cloned.1.call-update) | async-done | bytes 8388624 | tf_op jit(solution)/shard_map/all_gather | solution.py:132
  517.0 11.6 %fusion.50 = bf16[640,512]{0,1:T(8,128)(2,1)} fusion(bf16[8192,512]{1,0:T(8,128)(2,1)} %all-gather.7.cloned.1.call-done, bf16[640,8192]{1,0:T(8,128)(2,1)} %all-gather.5.cloned.1.call-done, f32[8192]{0:T(1024)S(1)} %copy-done.6, f32[640]{0:T(1024)S(1)} %add_rsqrt_fusion), kind=kOutput, calls=%fused_computation.57 | convolution fusion | flops 5385093120 | bytes 19565056 | tf_op jit(solution)/shard_map/dot_general | solution.py:139
  528.7 156.2 %all-gather.11.cloned.1.call-done = bf16[8192,2048]{1,0:T(8,128)(2,1)} async-done(((bf16[512,2048]{1,0:T(8,128)(2,1)}), bf16[8192,2048]{1,0:T(8,128)(2,1)}) %all-gather.11.cloned.1.call-update) | async-done | bytes 33554448 | tf_op jit(solution)/shard_map/all_gather | solution.py:130
  684.9 30.1 %fusion.24 = f32[640,2048]{1,0:T(8,128)} fusion(bf16[8192,2048]{1,0:T(8,128)(2,1)} %all-gather.11.cloned.1.call-done, bf16[640,8192]{1,0:T(8,128)(2,1)} %all-gather.5.cloned.1.call-done, f32[8192]{0:T(1024)S(1)} %copy-done.6, f32[640]{0:T(1024)S(1)} %add_rsqrt_fusion), kind=kOutput, calls=%fused_computation.41 | convolution fusion | flops 21491875840 | bytes 49318400 | tf_op jit(solution)/shard_map/dot_general | solution.py:139
  715.0 5.9 copy.48
  720.9 7.6 reshape.125
  728.5 4.5 slice_negate_fusion
  733.0 4.9 copy.49
  737.9 3.7 copy.50
  741.6 7.2 fusion.15
  748.8 10.3 %fusion.89 = f32[4,4,640]{2,1,0:T(4,128)S(1)} fusion(pred[640,640]{0,1:T(8,128)(4,1)} %fusion.43, bf16[640,4,128,1]{2,0,3,1:T(8,128)(2,1)} %fusion.57, bf16[640,4,4,128]{3,0,2,1:T(8,128)(2,1)S(1)} %fusion.15), kind=kOutput, calls=%fused_computation.106 | convolution fusion | flops 1703936640 | bytes 3727360 | tf_op jit(solution)/shard_map/sub | solution.py:62
  759.1 13.5 %fusion.40 = bf16[4,128,4,640]{3,1,2,0:T(8,128)(2,1)} fusion(bf16[640,4,128,1]{0,2,3,1:T(8,128)(2,1)S(1)} %bitcast.76, f32[4,4,640]{2,1,0:T(4,128)S(1)} %fusion.89, pred[640,640]{0,1:T(8,128)(4,1)} %fusion.43, bf16[640,4,128,1]{2,0,3,1:T(8,128)(2,1)} %fusion.57, bf16[640,4,4,128]{3,0,2,1:T(8,128)(2,1)S(1)} %fusion.15), kind=kOutput, calls=%fused_computation.51 | convolution fusion | flops 3389532672 | bytes 7004160 | tf_op jit(solution)/shard_map/grqk,kgd->qgrd/dot_general | solution.py:64
  772.6 4.4 copy.52
  777.0 29.5 %reduce-scatter.7.cloned.1.call-done = f32[72,2152]{1,0:T(8,128)} async-done(((f32[1152,2152]{1,0:T(8,128)}), f32[72,2152]{1,0:T(8,128)}) %reduce-scatter.7.cloned.1.call-update) | async-done | bytes 619792
  806.5 120.8 %reduce-scatter.9.cloned.1.call-done = f32[72,2152]{1,0:T(8,128)} async-done(((f32[1152,2152]{1,0:T(8,128)}), f32[72,2152]{1,0:T(8,128)}) %reduce-scatter.9.cloned.1.call-update) | async-done | bytes 619792
  (74 shorter events, 24.1 us)
Async XLA Ops:
  7.2 87.9 %all-reduce.4.cloned.1.call-start = ((), (), s32[]{:S(2)}) async-start(), calls=%async_computation.3 | async-start | bytes 4718592 | tf_op jit(solution)/shard_map/psum | solution.py:98
  8.7 9.8 %slice-start.1 = ((s8[4958208]{0:T(1024)(128)(4,1)}), s8[4194304]{0:T(1024)(128)(4,1)S(1)}, s32[]{:S(2)}) async-start(s8[4958208]{0:T(1024)(128)(4,1)} %bitcast.74), calls=%async_computation.11 | async-start | bytes 8388608
  10.6 7.9 slice-start.2
  16.4 2.1 copy-start.11
  18.6 5.0 copy-start.4
  18.6 5.1 copy-start.1
  18.6 76.5 %copy-start = (bf16[512,1152]{1,0:T(8,128)(2,1)S(1)}, bf16[512,1152]{1,0:T(8,128)(2,1)}, u32[]{:S(2)}) copy-start(bf16[512,1152]{1,0:T(8,128)(2,1)} %param.17) | copy-start | bytes 3538948
  18.6 76.5 %copy-start.7 = (f32[4096]{0:T(1024)S(1)}, f32[4096]{0:T(1024)}, u32[]{:S(2)}) copy-start(f32[4096]{0:T(1024)} %param.23) | copy-start | bytes 49156
  117.8 6.1 copy-start.2
  117.8 83.5 %all-to-all-start = ((bf16[16,32,4096]{2,1,0:T(8,128)(2,1)}), bf16[16,32,4096]{2,1,0:T(8,128)(2,1)}, u32[]{:S(2)}, u32[]{:S(2)}) async-start(bf16[16,32,4096]{2,1,0:T(8,128)(2,1)} %bitcast.69), calls=%async_computation | async-start | bytes 8388608 | tf_op jit(solution)/shard_map/all_to_all | solution.py:118
  123.6 240.7 %all-gather.5.cloned.1.call-start = ((), (), s32[]{:S(2)}) async-start(), calls=%async_computation.4 | async-start | bytes 15728640 | tf_op jit(solution)/shard_map/all_gather | solution.py:134
  213.8 3.9 slice-start
  220.6 2.1 copy-start.5
  220.6 2.1 copy-start.8
  220.6 2.1 copy-start.9
  220.6 221.0 %all-gather.9.cloned.1.call-start = ((), (), s32[]{:S(2)}) async-start(), calls=%async_computation.6 | async-start | bytes 8912896 | tf_op jit(solution)/shard_map/all_gather | solution.py:131
  221.3 295.7 %all-gather.7.cloned.1.call-start = ((), (), s32[]{:S(2)}) async-start(), calls=%async_computation.5 | async-start | bytes 8912896 | tf_op jit(solution)/shard_map/all_gather | solution.py:132
  221.9 463.0 %all-gather.11.cloned.1.call-start = ((), (), s32[]{:S(2)}) async-start(), calls=%async_computation.7 | async-start | bytes 35651584 | tf_op jit(solution)/shard_map/all_gather | solution.py:130
  222.5 584.0 %reduce-scatter.7.cloned.1.call-start = ((), (), s32[]{:S(2)}) async-start(), calls=%async_computation.8 | async-start | bytes 10653696
  237.3 690.0 %reduce-scatter.9.cloned.1.call-start = ((), (), s32[]{:S(2)}) async-start(), calls=%async_computation.9 | async-start | bytes 10653696
  248.7 0.7 copy-start.3
  252.2 189.4 %copy-start.6 = (f32[8192]{0:T(1024)S(1)}, f32[8192]{0:T(1024)}, u32[]{:S(2)}) copy-start(f32[8192]{0:T(1024)} %param.29) | copy-start | bytes 98308
  748.8 10.3 %copy-start.10 = (bf16[640,512]{0,1:T(8,128)(2,1)S(1)}, bf16[640,512]{0,1:T(8,128)(2,1)}, u32[]{:S(2)}) copy-start(bf16[640,512]{0,1:T(8,128)(2,1)} %fusion.50) | copy-start | bytes 1966084
Sparse Core Ops, SparseCore 0:
  23.7 71.3 all-reduce.3
  220.7 143.5 all-gather.4
  366.7 74.8 all-gather.8
  443.9 73.1 all-gather.6
  518.6 166.2 all-gather.10
  690.1 116.4 reduce-scatter.6
  811.8 115.4 reduce-scatter.8
where the time goes:
time: 944 us; the launch traced here: 935 us
  waiting for transfers between devices  697 us (74%)
  matrix products  135 us (14%)
  local copies, waits for them, and re-layouts  48.5 us (5%)
  other arithmetic  32.9 us (3%)
  between operations  14.8 us (2%)
    all_gather x1, waiting for transfers between devices, body(): lax.all_gather(q_weight, 'dp', axis=0, tiled=True)  156 us
    unnamed x9, waiting for transfers between devices  152 us
    all_gather x1, waiting for transfers between devices, body(): lax.all_gather(stream, 'mp', axis=1, tiled=True).astype(jnp.float32)  112 us
    all_to_all x1, waiting for transfers between devices, body(): lax.all_to_all(outbound, 'dp', split_axis=0, concat_axis=0, tiled=True)  77 us
    all_gather x1, waiting for transfers between devices, body(): lax.all_gather(k_weight, 'dp', axis=0, tiled=True)  71.2 us
    psum x1, waiting for transfers between devices, body(): lax.psum(jnp.dot(hidden_units, reduce_weight, preferred_element_type=jnp....  71.2 us
    dot_general x3, matrix products, body(): jnp.dot(scaled_piece, full_weights[number], preferred_element_type=jnp.fl...  58 us
    all_gather x1, waiting for transfers between devices, body(): lax.all_gather(v_weight, 'dp', axis=0, tiled=True)  57 us
  transfers between devices with their start and end apart: 8, of which 8 were waited for; matrix products, arithmetic and copies ran while one was open for 17% of the time, Pallas kernels for 0%

commit v1 on v0

v1 whole, which is shorter than its diff:
```python
import math

import jax
import jax.numpy as jnp
from jax import lax
from jax.experimental import pallas as pl
from jax.experimental.pallas import tpu as pltpu
from jax.sharding import PartitionSpec as P

D = 8192
HEAD = 128
TILE_ROWS = 32


def encoder_front(tiles, norm_gain, norm_bias, expand_weight):
    values = tiles.astype(jnp.float32)
    center = values - jnp.mean(values, axis=1, keepdims=True)
    variance = jnp.mean(center * center, axis=1, keepdims=True)
    normed = (center * lax.rsqrt(variance + 1e-06) * norm_gain + norm_bias).astype(jnp.bfloat16)
    pre_act = jnp.dot(normed, expand_weight, preferred_element_type=jnp.float32)
    hidden_units = jax.nn.gelu(pre_act, approximate=True).astype(jnp.bfloat16)
    return (normed, pre_act, hidden_units)


def gelu_slope(pre_act):
    factor = math.sqrt(2.0 / math.pi)
    inner = factor * (pre_act + 0.044715 * pre_act**3)
    tangent = jnp.tanh(inner)
    return 0.5 * (1.0 + tangent) + 0.5 * pre_act * (1.0 - tangent * tangent) * factor * (
        1.0 + 3.0 * 0.044715 * pre_act * pre_act
    )


def segment_positions(segments):
    count = segments.shape[0]
    index = jnp.arange(count, dtype=jnp.int32)
    same = segments[:, None] == segments[None, :]
    first = jnp.min(jnp.where(same, index[None, :], count), axis=1)
    return index - first


def rope_tables(positions):
    half = HEAD // 2
    freq = 1000000.0 ** (-(jnp.arange(half, dtype=jnp.float32) * 2.0 / HEAD))
    angle = positions.astype(jnp.float32)[:, None] * freq[None, :]
    cosine, sine = jnp.cos(angle), jnp.sin(angle)
    return (
        jnp.concatenate([cosine, cosine], axis=1),
        jnp.concatenate([-sine, sine], axis=1),
    )


def attention_kernel(q_ref, k_ref, v_ref, inv_ref, cos_ref, sin_ref, row_ref, col_ref, out_ref):
    count = q_ref.shape[0]
    inverse = inv_ref[...]
    cosine = cos_ref[...]
    sine = sin_ref[...]

    def turn(raw):
        raw = raw * inverse
        return (raw * cosine + pltpu.roll(raw, HEAD // 2, 1) * sine).astype(jnp.bfloat16)

    keys = turn(k_ref[...])
    values = (v_ref[...] * inverse).astype(jnp.bfloat16)
    rows = lax.broadcasted_iota(jnp.int32, (count, count), 0)
    columns = lax.broadcasted_iota(jnp.int32, (count, count), 1)
    allowed = (columns <= rows) & (row_ref[...] == col_ref[...])
    for head in range(q_ref.shape[1] // HEAD):
        span = slice(head * HEAD, (head + 1) * HEAD)
        queries = turn(q_ref[:, span])
        scores = lax.dot_general(
            queries, keys, (((1,), (1,)), ((), ())), preferred_element_type=jnp.float32
        ) * (1.0 / math.sqrt(HEAD))
        scores = jnp.where(allowed, scores, -1e30)
        weights = jnp.exp(scores - jnp.max(scores, axis=1, keepdims=True))
        probs = (weights * (1.0 / jnp.sum(weights, axis=1, keepdims=True))).astype(jnp.bfloat16)
        out_ref[:, span] = jnp.dot(probs, values, preferred_element_type=jnp.float32).astype(
            jnp.bfloat16
        )


def attend(raw, q_cols, kv_cols, inverse, positions, segments):
    count = raw.shape[0]
    groups = kv_cols // HEAD
    wide = q_cols // groups
    cosine, sine = rope_tables(positions)
    q_blocks = q_cols // HEAD
    whole = lambda g: (0, 0)
    return pl.pallas_call(
        attention_kernel,
        grid=(groups,),
        in_specs=[
            pl.BlockSpec((count, wide), lambda g: (0, g)),
            pl.BlockSpec((count, HEAD), lambda g: (0, q_blocks + g)),
            pl.BlockSpec((count, HEAD), lambda g: (0, q_blocks + groups + g)),
            pl.BlockSpec((count, 1), whole),
            pl.BlockSpec((count, HEAD), whole),
            pl.BlockSpec((count, HEAD), whole),
            pl.BlockSpec((count, 1), whole),
            pl.BlockSpec((1, count), whole),
        ],
        out_specs=pl.BlockSpec((count, wide), lambda g: (0, g)),
        out_shape=jax.ShapeDtypeStruct((count, q_cols), jnp.bfloat16),
        compiler_params=pltpu.CompilerParams(vmem_limit_bytes=40 * 1024 * 1024),
        cost_estimate=pl.CostEstimate(
            flops=4 * count * count * q_cols,
            bytes_accessed=6 * count * q_cols,
            transcendentals=count * count * (q_cols // HEAD),
        ),
    )(
        raw, raw, raw, inverse[:, None], cosine, sine, segments[:, None], segments[None, :]
    )


def swap_mp(values):
    return lax.ppermute(values, "mp", [(0, 1), (1, 0)])


def sum_mp(partial):
    if lax.axis_size("mp") != 2:
        return lax.psum(partial, "mp")
    return partial + swap_mp(partial.astype(jnp.bfloat16)).astype(jnp.float32)


def gather_mp(top, tail):
    if lax.axis_size("mp") != 2:
        return lax.all_gather(jnp.concatenate([top, tail], axis=0), "mp", axis=1, tiled=True)
    other = jnp.concatenate([swap_mp(top), swap_mp(tail)], axis=0)
    own = jnp.concatenate([top, tail], axis=0)
    first = lax.axis_index("mp") == 0
    return jnp.concatenate(
        [jnp.where(first, own, other), jnp.where(first, other, own)], axis=1
    )


def sum_scatter(values):
    size = lax.axis_size("dp")
    me = lax.axis_index("dp")
    width = values.shape[1]
    rows = values.shape[0] // size
    total = values.reshape(size, rows, width)
    step = 1
    while step < size:
        pairs = total.reshape(total.shape[0] // 2, 2, rows, width)
        bit = (me // step) % 2
        mine = jnp.where(bit == 0, pairs[:, 0], pairs[:, 1])
        other = jnp.where(bit == 0, pairs[:, 1], pairs[:, 0]).astype(jnp.bfloat16)
        arrived = lax.ppermute(other, "dp", [(i, i ^ step) for i in range(size)])
        total = mine + arrived.astype(jnp.float32)
        step *= 2
    return total.reshape(rows, width)


def body(
    tiles,
    norm_gain,
    norm_bias,
    expand_weight,
    reduce_weight,
    projector,
    projector_bias,
    tile_counts,
    tile_owner,
    tile_slot,
    segment_ids,
    text_embed,
    input_gain,
    q_weight,
    k_weight,
    v_weight,
    feature_grad,
):
    group_size = lax.axis_size("dp")
    my_index = lax.axis_index("dp")
    slot_count = tile_owner.shape[1]
    tile_rows = TILE_ROWS
    enc_rows = tiles.shape[0]
    full_weights = lax.all_gather(
        jnp.concatenate([q_weight, k_weight, v_weight], axis=1), "dp", axis=0, tiled=True
    )
    totals = jnp.sum(tile_counts, axis=1)
    slot_ids = jnp.arange(slot_count, dtype=jnp.int32)
    live_all = slot_ids[None, :] < totals[:, None]
    my_live = lax.dynamic_index_in_dim(live_all, my_index, 0, keepdims=False)
    my_owner = lax.dynamic_index_in_dim(tile_owner, my_index, 0, keepdims=False)
    normed, pre_act, hidden_units = encoder_front(tiles, norm_gain, norm_bias, expand_weight)
    partial = jnp.dot(hidden_units, reduce_weight, preferred_element_type=jnp.float32)
    summed = sum_mp(partial)
    enc_out = (tiles.astype(jnp.float32) + summed).astype(jnp.bfloat16)
    outgoing = (
        (jnp.arange(group_size, dtype=jnp.int32)[:, None] == my_owner[None, :]) & my_live[None, :]
    ).astype(jnp.bfloat16)
    match = (tile_owner == my_index) & live_all
    filled = jnp.any(match, axis=1)
    slot_used = jnp.sum(jnp.where(match, tile_slot, 0), axis=1)
    placing = (filled[None, :] & (slot_used[None, :] == slot_ids[:, None])).astype(jnp.bfloat16)
    flat_tiles = enc_out.reshape(slot_count, -1)
    outbound = (
        jnp.dot(outgoing, flat_tiles, preferred_element_type=jnp.float32)
        .astype(jnp.bfloat16)
        .reshape(group_size, tile_rows, -1)
    )
    inbound = lax.all_to_all(outbound, "dp", split_axis=0, concat_axis=0, tiled=True)
    placed = (
        jnp.dot(placing, inbound.reshape(group_size, -1), preferred_element_type=jnp.float32)
        .astype(jnp.bfloat16)
        .reshape(enc_rows, -1)
    )
    images = (
        jnp.dot(placed, projector, preferred_element_type=jnp.float32) + projector_bias
    ).astype(jnp.bfloat16)
    is_image = jnp.repeat(jnp.sum(placing, axis=1) > 0, tile_rows)[:, None]
    top = jnp.where(is_image, images, text_embed[:enc_rows])
    piece_values = gather_mp(top, text_embed[enc_rows:]).astype(jnp.float32)
    scaled = (piece_values * input_gain).astype(jnp.bfloat16)
    squares = jnp.sum(piece_values * piece_values, axis=1)
    inverse = lax.rsqrt(squares / D + 1e-06)
    segments = segment_ids[0]
    positions = segment_positions(segments)
    scaled, inverse = lax.optimization_barrier((scaled, inverse))
    raw = jnp.dot(scaled, full_weights, preferred_element_type=jnp.float32)
    context = attend(raw, q_weight.shape[1], k_weight.shape[1], inverse, positions, segments)
    live_rows = jnp.repeat(my_live, tile_rows)[:, None]
    cotangent = jnp.where(live_rows, feature_grad, jnp.zeros_like(feature_grad))
    hidden_grad = lax.dot_general(
        cotangent, reduce_weight, (((1,), (1,)), ((), ())), preferred_element_type=jnp.float32
    )
    act_grad = (hidden_grad * gelu_slope(pre_act)).astype(jnp.bfloat16)
    reduce_grad_t = lax.dot_general(
        cotangent, hidden_units, (((0,), (0,)), ((), ())), preferred_element_type=jnp.float32
    )
    expand_grad = lax.dot_general(
        normed, act_grad, (((0,), (0,)), ((), ())), preferred_element_type=jnp.float32
    )
    expand_grad, reduce_grad_t = sum_scatter(expand_grad), sum_scatter(reduce_grad_t)
    return (context, expand_grad, reduce_grad_t)


def solution(mesh):
    in_specs = (
        P("dp", None),
        P(),
        P(),
        P(None, "mp"),
        P("mp", None),
        P(None, "mp"),
        P("mp"),
        P(),
        P(),
        P(),
        P("dp", None),
        P("dp", "mp"),
        P(),
        P("dp", "mp"),
        P("dp", "mp"),
        P("dp", "mp"),
        P("dp", None),
    )
    out_specs = (P("dp", "mp"), P("dp", "mp"), P("dp", "mp"))
    return jax.shard_map(body, mesh=mesh, in_specs=in_specs, out_specs=out_specs, check_vma=False)
```

time: 944 us -> 391 us (0.41)
  waiting for transfers between devices: 697 us -> 191 us
  matrix products: 135 us -> 80.9 us
  local copies, waits for them, and re-layouts: 48.5 us -> 16.2 us
  Pallas kernels: 0 us -> 15.8 us
  other arithmetic: 32.9 us -> 48.4 us
  starting transfers between devices: 6.7 us -> 21.2 us
    all_gather x4 -> x1, waiting for transfers between devices: 397 us -> 22.5 us  [body(): lax.all_gather(jnp.concatenate([q_weight, k_weight, v_weight], axis=1), '...]
    unnamed x9 -> x1, waiting for transfers between devices: 152 us -> 0.02 us
    ppermute x0 -> x11, waiting for transfers between devices: none -> 143 us  [the longest x8 121 us: sum_scatter(): arrived = lax.ppermute(other, 'dp', [(i, i ^ step) for i in range(size)])]
    psum x1 -> x0, waiting for transfers between devices: 71.2 us -> none  [body(): lax.psum(jnp.dot(hidden_units, reduce_weight, preferred_element_type=jnp....]
    all_to_all x1, waiting for transfers between devices: 77 us -> 25 us  [body(): lax.all_to_all(outbound, 'dp', split_axis=0, concat_axis=0, tiled=True)]
    dot_general x5 -> x2, matrix products: 81.7 us -> 48 us  [the longest x1 38.8 us: body(): raw = jnp.dot(scaled, full_weights, preferred_element_type=jnp.float32)]
    add x0 -> x4, other arithmetic: none -> 16.8 us  [sum_scatter(): total = mine + arrived.astype(jnp.float32)]
    pallas_call x0 -> x1, Pallas kernels: none -> 15.8 us  [attend(): pl.pallas_call(attention_kernel, grid=(groups,), in_specs=[pl.BlockSpec((...]
  transfers between devices with their start and end apart: 8 -> 13, of which waited for: 8 -> 8; matrix products, arithmetic and copies ran while one was open for 17% -> 25% of each run, Pallas kernels for 0% -> 0%
where the time goes in v1:
time: 391 us; the launch traced here: 388 us
  waiting for transfers between devices  191 us (49%)
  matrix products  80.9 us (21%)
  other arithmetic  48.4 us (12%)
  starting transfers between devices  21.2 us (5%)
  local copies, waits for them, and re-layouts  16.2 us (4%)
  Pallas kernels  15.8 us (4%)
  between operations  14.7 us (4%)
    ppermute x8, waiting for transfers between devices, sum_scatter(): arrived = lax.ppermute(other, 'dp', [(i, i ^ step) for i in range(size)])  121 us
    dot_general x1, matrix products, body(): raw = jnp.dot(scaled, full_weights, preferred_element_type=jnp.float32)  38.8 us
    all_to_all x1, waiting for transfers between devices, body(): lax.all_to_all(outbound, 'dp', split_axis=0, concat_axis=0, tiled=True)  25 us
    all_gather x1, waiting for transfers between devices, body(): lax.all_gather(jnp.concatenate([q_weight, k_weight, v_weight], axis=1), '...  22.5 us
    ppermute x3, waiting for transfers between devices, swap_mp(): return lax.ppermute(values, 'mp', [(0, 1), (1, 0)])  22.1 us
    add x4, other arithmetic, sum_scatter(): total = mine + arrived.astype(jnp.float32)  16.8 us
    pallas_call x1, Pallas kernels, attend(): pl.pallas_call(attention_kernel, grid=(groups,), in_specs=[pl.BlockSpec((...  15.8 us
    dot_general x1, matrix products, body(): lax.dot_general(normed, act_grad, (((0,), (0,)), ((), ())), preferred_ele...  14.6 us
  transfers between devices with their start and end apart: 13, of which 8 were waited for; matrix products, arithmetic and copies ran while one was open for 25% of the time, Pallas kernels for 0%

profile of v1, /device:TPU:0, one launch (start us, length us, event | category | flops | bytes accessed | tf_op | source)
XLA Modules:
  0.0 388.0 jit_solution(2997656799909522201)
XLA Ops:
  7.2 3.2 pad_maximum_fusion.2
  12.5 6.0 %fusion.56 = f32[512,2152]{0,1:T(8,128)S(1)} fusion(bf16[1152,2152]{0,1:T(8,128)(2,1)} %param.20, bf16[512,1152]{1,0:T(8,128)(2,1)S(1)} %copy-done.4, f32[1152]{0:T(1024)S(1)} %copy-done.13, f32[1152]{0:T(1024)S(1)} %copy-done.14, f32[512]{0:T(512)S(1)} %add_rsqrt_fusion.1, f32[512]{0:T(512)S(1)} %broadcast_multiply_fusion), kind=kOutput, calls=%fused_computation.113 | convolution fusion | flops 2542141440 | bytes 10558464 | tf_op jit(solution)/shard_map/dot_general | solution.py:20
  18.5 3.3 fusion.33
  21.8 3.7 copy-done.3
  25.6 1.9 fusion.16
  28.0 14.6 %fusion.28 = f32[1152,2152]{1,0:T(8,128)} fusion(bf16[2152,1152]{1,0:T(8,128)(2,1)} %param.21, f32[512,2152]{0,1:T(8,128)} %copy-done.15, bf16[512,1152]{1,0:T(8,128)(2,1)S(1)} %copy-done.11, pred[512]{0:T(512)(128)(4,1)S(1)} %broadcast_in_dim.73, bf16[512,1152]{1,0:T(8,128)(2,1)S(1)} %copy-done.4, f32[1152]{0:T(1024)S(1)} %copy-done.13, ...), kind=kOutput, calls=%fused_computation.66 | convolution fusion | flops 5102268416 | bytes 21655040 | tf_op jit(solution)/shard_map/dot_general | solution.py:232
  42.6 6.0 %fusion.15 = bf16[8,72,2152]{2,1,0:T(8,128)(2,1)} fusion(f32[8,2,72,2152]{3,2,1,0:T(8,128)} %bitcast.159, pred[]{:T(512)S(6)} %eq.102), kind=kLoop, calls=%fused_computation.37 | loop fusion | flops 1239552 | bytes 7437313 | tf_op jit(solution)/shard_map/convert_element_type | solution.py:147
  48.8 8.1 %fusion.60 = (bf16[512,1152]{1,0:T(8,128)(2,1)}, f32[512,1152]{1,0:T(8,128)}) fusion(bf16[2152,1152]{1,0:T(8,128)(2,1)} %param.21, f32[512,2152]{0,1:T(8,128)S(1)} %copy-done.16), kind=kOutput, calls=%fused_computation.116 | convolution fusion | flops 2549108736 | bytes 12904448 | tf_op jit(solution)/shard_map/dot_general | solution.py:187
  56.9 3.2 collective-permute-start
  60.1 2.3 slice.71
  65.0 22.1 %collective-permute-done = bf16[512,1152]{1,0:T(8,128)(2,1)S(1)} collective-permute-done((bf16[512,1152]{1,0:T(8,128)(2,1)}, bf16[512,1152]{1,0:T(8,128)(2,1)S(1)}, u32[]{:S(2)}, u32[]{:S(2)}) %collective-permute-start) | collective-permute-done | bytes 1179680 | tf_op jit(solution)/shard_map/ppermute | solution.py:116
  88.1 1.7 fusion.21
  92.1 7.1 %all-to-all-start = ((bf16[16,32,1152]{2,1,0:T(8,128)(2,1)}), bf16[16,32,1152]{2,1,0:T(8,128)(2,1)S(1)}, u32[]{:S(2)}, u32[]{:S(2)}) async-start(bf16[16,32,1152]{2,1,0:T(8,128)(2,1)} %bitcast.48), calls=%async_computation | async-start | bytes 2359296 | tf_op jit(solution)/shard_map/all_to_all | solution.py:203
  99.2 5.4 %fusion.3 = f32[8,72,2152]{2,1,0:T(8,128)S(1)} fusion(bf16[8,72,2152]{2,1,0:T(8,128)(2,1)} %collective-permute-done.7, f32[8,2,72,2152]{3,2,1,0:T(8,128)} %bitcast.162, pred[]{:T(512)S(6)} %eq.102), kind=kLoop, calls=%fused_computation.16 | loop fusion | flops 3718656 | bytes 17353728 | tf_op jit(solution)/shard_map/add | solution.py:149
  106.1 1.9 collective-permute-start.8
  108.0 5.2 %bitcast_add_fusion = f32[8,72,2152]{2,1,0:T(8,128)S(1)} fusion(bf16[8,72,2152]{2,1,0:T(8,128)(2,1)} %collective-permute-done.3, f32[8,2,72,2152]{3,2,1,0:T(8,128)} %bitcast.160, pred[]{:T(512)S(6)} %eq.102), kind=kLoop, calls=%fused_computation.17 | loop fusion | flops 3718656 | bytes 17353728 | tf_op jit(solution)/shard_map/add | solution.py:149
  113.3 2.3 copy-done.1
  118.2 25.0 %all-to-all-done = bf16[16,32,1152]{2,1,0:T(8,128)(2,1)S(1)} async-done(((bf16[16,32,1152]{2,1,0:T(8,128)(2,1)}), bf16[16,32,1152]{2,1,0:T(8,128)(2,1)S(1)}, u32[]{:S(2)}, u32[]{:S(2)}) %all-to-all-start) | async-done | bytes 1179680 | tf_op jit(solution)/shard_map/all_to_all | solution.py:203
  145.4 9.2 %fusion.4 = bf16[512,4096]{1,0:T(8,128)(2,1)S(1)} fusion(bf16[512,1152]{1,0:T(8,128)(2,1)} %reshape.208, bf16[1152,4096]{1,0:T(8,128)(2,1)} %param.22, bf16[640,4096]{1,0:T(8,128)(2,1)} %param.28, f32[4096]{0:T(1024)S(1)} %copy-done.12, pred[512]{0:T(512)(128)(4,1)S(1)} %broadcast_in_dim.67), kind=kOutput, calls=%fused_computation.20 | convolution fusion | flops 4838129664 | bytes 19022336 | tf_op jit(solution)/shard_map/dot_general | solution.py:210
  154.6 1.5 collective-permute-start.1
  156.2 16.2 %collective-permute-done.8 = bf16[4,72,2152]{2,1,0:T(8,128)(2,1)S(1)} collective-permute-done((bf16[4,72,2152]{2,1,0:T(8,128)(2,1)}, bf16[4,72,2152]{2,1,0:T(8,128)(2,1)S(1)}, u32[]{:S(2)}, u32[]{:S(2)}) %collective-permute-start.8) | collective-permute-done | bytes 1239584 | tf_op jit(solution)/shard_map/ppermute | solution.py:148
  172.3 3.0 bitcast_add_fusion.1
  175.5 50.5 %collective-permute-done.4 = bf16[4,72,2152]{2,1,0:T(8,128)(2,1)} collective-permute-done((bf16[4,72,2152]{2,1,0:T(8,128)(2,1)}, bf16[4,72,2152]{2,1,0:T(8,128)(2,1)}, u32[]{:S(2)}, u32[]{:S(2)}) %collective-permute-start.4) | collective-permute-done | bytes 1239584 | tf_op jit(solution)/shard_map/ppermute | solution.py:148
  226.0 3.2 bitcast_add_fusion.2
  229.6 3.9 collective-permute-start.10
  233.5 32.5 %collective-permute-done.5 = bf16[2,72,2152]{2,1,0:T(8,128)(2,1)S(1)} collective-permute-done((bf16[2,72,2152]{2,1,0:T(8,128)(2,1)S(1)}, bf16[2,72,2152]{2,1,0:T(8,128)(2,1)S(1)}, u32[]{:S(2)}, u32[]{:S(2)}) %collective-permute-start.5) | collective-permute-done | bytes 619808 | tf_op jit(solution)/shard_map/ppermute | solution.py:148
  268.9 21.5 %collective-permute-done.6 = bf16[1,72,2152]{2,1,0:T(8,128)(2,1)S(1)} collective-permute-done((bf16[1,72,2152]{2,1,0:T(8,128)(2,1)S(1)}, bf16[1,72,2152]{2,1,0:T(8,128)(2,1)S(1)}, u32[]{:S(2)}, u32[]{:S(2)}) %collective-permute-start.6) | collective-permute-done | bytes 309920 | tf_op jit(solution)/shard_map/ppermute | solution.py:148
  293.2 4.4 %broadcast_select_fusion.1 = (bf16[640,4096]{1,0:T(8,128)(2,1)S(1)}, bf16[640,4096]{1,0:T(8,128)(2,1)S(1)}) fusion(bf16[640,4096]{1,0:T(8,128)(2,1)S(1)} %constant_dynamic-update-slice_fusion, pred[]{:T(512)S(6)} %eq.85, bf16[128,4096]{1,0:T(8,128)(2,1)} %slice.71, bf16[512,4096]{1,0:T(8,128)(2,1)S(1)} %fusion.4), kind=kLoop, calls=%fused_computation.12 | loop fusion | flops 15728640 | bytes 20971520 | tf_op jit(solution)/shard_map/jit(_where)/select_n | solution.py:132
  297.6 6.0 %fusion.1 = (f32[640]{0:T(1024)S(1)}, bf16[640,8192]{1,0:T(8,128)(2,1)}) fusion(bf16[640,4096]{1,0:T(8,128)(2,1)S(1)} %get-tuple-element.12, bf16[640,4096]{1,0:T(8,128)(2,1)S(1)} %get-tuple-element.11, f32[8192]{0:T(1024)S(1)} %copy-done.7), kind=kLoop, calls=%fused_computation.5 | loop fusion | flops 41942400 | bytes 21006848 | tf_op jit(solution)/shard_map/reduce_sum | solution.py:216
  303.7 22.5 %all-gather.2.cloned.1.call-done = bf16[8192,3072]{1,0:T(8,128)(2,1)} async-done(((bf16[512,3072]{1,0:T(8,128)(2,1)}), bf16[8192,3072]{1,0:T(8,128)(2,1)}) %all-gather.2.cloned.1.call-update) | async-done | bytes 50331664 | tf_op jit(solution)/shard_map/all_gather | solution.py:178
  326.3 38.8 %fusion.61.q_ref.k_ref.v_ref = f32[640,3072]{1,0:T(8,128)S(1)} fusion(bf16[640,8192]{1,0:T(8,128)(2,1)} %get-tuple-element.5, bf16[8192,3072]{1,0:T(8,128)(2,1)} %all-gather.2.cloned.1.call-done), kind=kOutput, calls=%fused_computation.117 | convolution fusion | flops 32212254720 | bytes 68681728 | tf_op jit(solution)/shard_map/dot_general | solution.py:221
  365.1 15.8 %shard_map.184 = bf16[640,2048]{1,0:T(8,128)(2,1)} custom-call(f32[640,3072]{1,0:T(8,128)S(1)} %fusion.61.q_ref.k_ref.v_ref, f32[640,3072]{1,0:T(8,128)S(1)} %fusion.61.q_ref.k_ref.v_ref, f32[640,3072]{1,0:T(8,128)S(1)} %fusion.61.q_ref.k_ref.v_ref, f32[640,1]{1,0:T(8,128)S(1)} %broadcast_in_dim.76.inv_ref, f32[640,128]{1,0:T(8,128)S(1)} %get-tuple-element.19.cos_ref, ...), custom_call_target="tpu_custom_call" | custom-call | flops 3355443200 | bytes 7864320 | tf_op jit(solution)/shard_map/pallas_call | solution.py:89
  (89 shorter events, 21.0 us)
Async XLA Ops:
  7.2 319.1 %all-gather.2.cloned.1.call-start = ((), (), s32[]{:S(2)}) async-start(), calls=%async_computation.1 | async-start | bytes 53477376 | tf_op jit(solution)/shard_map/all_gather | solution.py:178
  10.4 0.7 copy-start.10
  10.4 0.7 copy-start.8
  10.5 1.3 copy-start.4
  10.5 2.0 copy-start.13
  10.5 2.0 copy-start.14
  12.5 6.0 %copy-start.11 = (bf16[512,1152]{1,0:T(8,128)(2,1)S(1)}, bf16[512,1152]{1,0:T(8,128)(2,1)}, u32[]{:S(2)}) copy-start(bf16[512,1152]{1,0:T(8,128)(2,1)} %param.33) | copy-start | bytes 3538948
  18.5 3.3 copy-start.15
  21.8 3.7 copy-start.3
  27.5 71.7 %collective-permute-start.7 = (bf16[8,72,2152]{2,1,0:T(8,128)(2,1)}, bf16[8,72,2152]{2,1,0:T(8,128)(2,1)}, u32[]{:S(2)}, u32[]{:S(2)}) collective-permute-start(bf16[8,72,2152]{2,1,0:T(8,128)(2,1)} %fusion.16), channel_id=1, source_target_pairs={{0,2},{2,0},{4,6},{6,4},{8,10},{10,8},{12,14},{14,12},{16,18},{18,... | collective-permute-start | bytes 7437320 | tf_op jit(solution)/shard_map/ppermute | solution.py:148
  42.6 6.3 %copy-start.16 = (f32[512,2152]{0,1:T(8,128)S(1)}, f32[512,2152]{0,1:T(8,128)}, u32[]{:S(2)}) copy-start(f32[512,2152]{0,1:T(8,128)} %copy-done.15) | copy-start | bytes 13221892
  48.6 13.9 %copy-start.9 = (s32[16,16]{1,0:T(8,128)S(1)}, s32[16,16]{1,0:T(8,128)}, u32[]{:S(2)}) copy-start(s32[16,16]{1,0:T(8,128)} %param.26) | copy-start | bytes 3076
  48.6 14.3 %copy-start = (s32[1,640]{1,0:T(1,128)S(1)}, s32[1,640]{1,0:T(1,128)}, u32[]{:S(2)}) copy-start(s32[1,640]{1,0:T(1,128)} %col_ref.1) | copy-start | bytes 7684
  48.6 59.4 %collective-permute-start.3 = (bf16[8,72,2152]{2,1,0:T(8,128)(2,1)}, bf16[8,72,2152]{2,1,0:T(8,128)(2,1)}, u32[]{:S(2)}, u32[]{:S(2)}) collective-permute-start(bf16[8,72,2152]{2,1,0:T(8,128)(2,1)} %fusion.15), channel_id=1, source_target_pairs={{0,2},{2,0},{4,6},{6,4},{8,10},{10,8},{12,14},{14,12},{16,18},{18,... | collective-permute-start | bytes 7437320 | tf_op jit(solution)/shard_map/ppermute | solution.py:148
  56.9 30.2 %collective-permute-start = (bf16[512,1152]{1,0:T(8,128)(2,1)}, bf16[512,1152]{1,0:T(8,128)(2,1)S(1)}, u32[]{:S(2)}, u32[]{:S(2)}) collective-permute-start(bf16[512,1152]{1,0:T(8,128)(2,1)} %get-tuple-element.17), channel_id=1, source_target_pairs={{0,1},{1,0},{2,3},{3,2},{4,5},{5,4},{6,7},{7,6},{8,9},{9,8},{10,11... | collective-permute-start | bytes 3538952 | tf_op jit(solution)/shard_map/ppermute | solution.py:116
  62.5 229.4 %collective-permute-start.2 = (bf16[128,4096]{1,0:T(8,128)(2,1)}, bf16[128,4096]{1,0:T(8,128)(2,1)}, u32[]{:S(2)}, u32[]{:S(2)}) collective-permute-start(bf16[128,4096]{1,0:T(8,128)(2,1)} %slice.71), channel_id=1, source_target_pairs={{0,1},{1,0},{2,3},{3,2},{4,5},{5,4},{6,7},{7,6},{8,9},{9,8},{10,11... | collective-permute-start | bytes 3145736 | tf_op jit(solution)/shard_map/ppermute | solution.py:116
  63.1 25.1 %copy-start.5 = (f32[512,1152]{1,0:T(8,128)S(1)}, f32[512,1152]{1,0:T(8,128)}, u32[]{:S(2)}) copy-start(f32[512,1152]{1,0:T(8,128)} %get-tuple-element.18) | copy-start | bytes 7077892
  87.1 1.0 copy-start.6
  92.1 51.2 %all-to-all-start = ((bf16[16,32,1152]{2,1,0:T(8,128)(2,1)}), bf16[16,32,1152]{2,1,0:T(8,128)(2,1)S(1)}, u32[]{:S(2)}, u32[]{:S(2)}) async-start(bf16[16,32,1152]{2,1,0:T(8,128)(2,1)} %bitcast.48), calls=%async_computation | async-start | bytes 2359296 | tf_op jit(solution)/shard_map/all_to_all | solution.py:203
  104.6 3.4 copy-start.2
  106.1 66.3 %collective-permute-start.8 = (bf16[4,72,2152]{2,1,0:T(8,128)(2,1)}, bf16[4,72,2152]{2,1,0:T(8,128)(2,1)S(1)}, u32[]{:S(2)}, u32[]{:S(2)}) collective-permute-start(bf16[4,72,2152]{2,1,0:T(8,128)(2,1)} %fusion.23), channel_id=1, source_target_pairs={{0,4},{2,6},{4,0},{6,2},{8,12},{10,14},{12,8},{14,10},{16,20},{18,... | collective-permute-start | bytes 3718664 | tf_op jit(solution)/shard_map/ppermute | solution.py:148
  113.3 2.3 copy-start.1
  116.8 109.2 %collective-permute-start.4 = (bf16[4,72,2152]{2,1,0:T(8,128)(2,1)}, bf16[4,72,2152]{2,1,0:T(8,128)(2,1)}, u32[]{:S(2)}, u32[]{:S(2)}) collective-permute-start(bf16[4,72,2152]{2,1,0:T(8,128)(2,1)} %fusion.22), channel_id=1, source_target_pairs={{0,4},{2,6},{4,0},{6,2},{8,12},{10,14},{12,8},{14,10},{16,20},{18,... | collective-permute-start | bytes 3718664 | tf_op jit(solution)/shard_map/ppermute | solution.py:148
  143.2 2.2 copy-start.12
  154.6 136.7 %collective-permute-start.1 = (bf16[512,4096]{1,0:T(8,128)(2,1)S(1)}, bf16[512,4096]{1,0:T(8,128)(2,1)S(1)}, u32[]{:S(2)}, u32[]{:S(2)}) collective-permute-start(bf16[512,4096]{1,0:T(8,128)(2,1)S(1)} %fusion.4), channel_id=1, source_target_pairs={{0,1},{1,0},{2,3},{3,2},{4,5},{5,4},{6,7},{7,6},{8,9},{9,8},{10,11... | collective-permute-start | bytes 12582920 | tf_op jit(solution)/shard_map/ppermute | solution.py:116
  175.4 53.9 %collective-permute-start.9 = (bf16[2,72,2152]{2,1,0:T(8,128)(2,1)S(1)}, bf16[2,72,2152]{2,1,0:T(8,128)(2,1)S(1)}, u32[]{:S(2)}, u32[]{:S(2)}) collective-permute-start(bf16[2,72,2152]{2,1,0:T(8,128)(2,1)S(1)} %fusion.30), channel_id=1, source_target_pairs={{0,8},{2,10},{4,12},{6,14},{8,0},{10,2},{12,4},{14,6},{16,24},{18,... | collective-permute-start | bytes 1859336 | tf_op jit(solution)/shard_map/ppermute | solution.py:148
  229.3 36.7 %collective-permute-start.5 = (bf16[2,72,2152]{2,1,0:T(8,128)(2,1)S(1)}, bf16[2,72,2152]{2,1,0:T(8,128)(2,1)S(1)}, u32[]{:S(2)}, u32[]{:S(2)}) collective-permute-start(bf16[2,72,2152]{2,1,0:T(8,128)(2,1)S(1)} %fusion.29), channel_id=1, source_target_pairs={{0,8},{2,10},{4,12},{6,14},{8,0},{10,2},{12,4},{14,6},{16,24},{18,... | collective-permute-start | bytes 1859336 | tf_op jit(solution)/shard_map/ppermute | solution.py:148
  229.6 38.4 %collective-permute-start.10 = (bf16[1,72,2152]{2,1,0:T(8,128)(2,1)S(1)}, bf16[1,72,2152]{2,1,0:T(8,128)(2,1)S(1)}, u32[]{:S(2)}, u32[]{:S(2)}) collective-permute-start(bf16[1,72,2152]{2,1,0:T(8,128)(2,1)S(1)} %fusion.35), channel_id=1, source_target_pairs={{0,16},{2,18},{4,20},{6,22},{8,24},{10,26},{12,28},{14,30},{16,0},... | collective-permute-start | bytes 929672 | tf_op jit(solution)/shard_map/ppermute | solution.py:148
  266.3 24.2 %collective-permute-start.6 = (bf16[1,72,2152]{2,1,0:T(8,128)(2,1)S(1)}, bf16[1,72,2152]{2,1,0:T(8,128)(2,1)S(1)}, u32[]{:S(2)}, u32[]{:S(2)}) collective-permute-start(bf16[1,72,2152]{2,1,0:T(8,128)(2,1)S(1)} %fusion.34), channel_id=1, source_target_pairs={{0,16},{2,18},{4,20},{6,22},{8,24},{10,26},{12,28},{14,30},{16,0},... | collective-permute-start | bytes 929672 | tf_op jit(solution)/shard_map/ppermute | solution.py:148
  293.2 4.4 %copy-start.7 = (f32[8192]{0:T(1024)S(1)}, f32[8192]{0:T(1024)}, u32[]{:S(2)}) copy-start(f32[8192]{0:T(1024)} %param.29) | copy-start | bytes 98308
Sparse Core Ops, SparseCore 0:
  10.6 315.6 all-gather.1

commit v2 on v1

--- a/solution.py
+++ b/solution.py
@@ -133,14 +133,12 @@
     )
 
 
-def sum_scatter(values):
+def sum_scatter(total, low, high):
     size = lax.axis_size("dp")
     me = lax.axis_index("dp")
-    width = values.shape[1]
-    rows = values.shape[0] // size
-    total = values.reshape(size, rows, width)
-    step = 1
-    while step < size:
+    rows, width = total.shape[1:]
+    step = low
+    while step < high:
         pairs = total.reshape(total.shape[0] // 2, 2, rows, width)
         bit = (me // step) % 2
         mine = jnp.where(bit == 0, pairs[:, 0], pairs[:, 1])
@@ -148,7 +146,7 @@
         arrived = lax.ppermute(other, "dp", [(i, i ^ step) for i in range(size)])
         total = mine + arrived.astype(jnp.float32)
         step *= 2
-    return total.reshape(rows, width)
+    return total
 
 
 def body(
@@ -217,9 +215,6 @@
     inverse = lax.rsqrt(squares / D + 1e-06)
     segments = segment_ids[0]
     positions = segment_positions(segments)
-    scaled, inverse = lax.optimization_barrier((scaled, inverse))
-    raw = jnp.dot(scaled, full_weights, preferred_element_type=jnp.float32)
-    context = attend(raw, q_weight.shape[1], k_weight.shape[1], inverse, positions, segments)
     live_rows = jnp.repeat(my_live, tile_rows)[:, None]
     cotangent = jnp.where(live_rows, feature_grad, jnp.zeros_like(feature_grad))
     hidden_grad = lax.dot_general(
@@ -232,7 +227,19 @@
     expand_grad = lax.dot_general(
         normed, act_grad, (((0,), (0,)), ((), ())), preferred_element_type=jnp.float32
     )
-    expand_grad, reduce_grad_t = sum_scatter(expand_grad), sum_scatter(reduce_grad_t)
+    early = min(4, group_size)
+    reduce_part, expand_part = (
+        sum_scatter(grad.reshape(group_size, -1, grad.shape[1]), 1, early)
+        for grad in (reduce_grad_t, expand_grad)
+    )
+    scaled, inverse, full_weights, reduce_part, expand_part = lax.optimization_barrier(
+        (scaled, inverse, full_weights, reduce_part, expand_part)
+    )
+    raw = jnp.dot(scaled, full_weights, preferred_element_type=jnp.float32)
+    context = attend(raw, q_weight.shape[1], k_weight.shape[1], inverse, positions, segments)
+    reduce_grad_t, expand_grad = (
+        sum_scatter(part, early, group_size)[0] for part in (reduce_part, expand_part)
+    )
     return (context, expand_grad, reduce_grad_t)
 
 

time: 391 us -> 426 us (1.090)
  waiting for transfers between devices: 191 us -> 228 us
  local copies, waits for them, and re-layouts: 16.2 us -> 8.75 us
  other arithmetic: 48.4 us -> 52.8 us
  matrix products: 80.9 us -> 85.3 us
    all_gather x1, waiting for transfers between devices: 22.5 us -> 75.6 us  [body(): lax.all_gather(jnp.concatenate([q_weight, k_weight, v_weight], axis=1), '...]
    ppermute x3, waiting for transfers between devices: 22.1 us -> 0.01 us  [swap_mp(): return lax.ppermute(values, 'mp', [(0, 1), (1, 0)])]
    unnamed x37 -> x39, local copies, waits for them, and re-layouts: 9.96 us -> 3.3 us
    convert_element_type x8, other arithmetic: 11 us -> 17.5 us  [sum_scatter(): other = jnp.where(bit == 0, pairs[:, 1], pairs[:, 0]).astype(jnp.bfloat16)]
    ppermute x8, waiting for transfers between devices: 121 us -> 127 us  [sum_scatter(): arrived = lax.ppermute(other, 'dp', [(i, i ^ step) for i in range(size)])]
  transfers between devices with their start and end apart: 13 -> 13, of which waited for: 8 -> 6; matrix products, arithmetic and copies ran while one was open for 25% -> 33% of each run, Pallas kernels for 0% -> 4%
where the time goes in v2:
time: 426 us; the launch traced here: 423 us
  waiting for transfers between devices  228 us (54%)
  matrix products  85.3 us (20%)
  other arithmetic  52.8 us (12%)
  starting transfers between devices  17.8 us (4%)
  Pallas kernels  15.8 us (4%)
  between operations  14.6 us (3%)
  local copies, waits for them, and re-layouts  8.75 us (2%)
    ppermute x8, waiting for transfers between devices, sum_scatter(): arrived = lax.ppermute(other, 'dp', [(i, i ^ step) for i in range(size)])  127 us
    all_gather x1, waiting for transfers between devices, body(): lax.all_gather(jnp.concatenate([q_weight, k_weight, v_weight], axis=1), '...  75.6 us
    dot_general x1, matrix products, body(): raw = jnp.dot(scaled, full_weights, preferred_element_type=jnp.float32)  38.7 us
    all_to_all x1, waiting for transfers between devices, body(): lax.all_to_all(outbound, 'dp', split_axis=0, concat_axis=0, tiled=True)  26.2 us
    convert_element_type x8, other arithmetic, sum_scatter(): other = jnp.where(bit == 0, pairs[:, 1], pairs[:, 0]).astype(jnp.bfloat16)  17.5 us
    pallas_call x1, Pallas kernels, attend(): pl.pallas_call(attention_kernel, grid=(groups,), in_specs=[pl.BlockSpec((...  15.8 us
    add x4, other arithmetic, sum_scatter(): total = mine + arrived.astype(jnp.float32)  15.4 us
    dot_general x1, matrix products, body(): lax.dot_general(normed, act_grad, (((0,), (0,)), ((), ())), preferred_ele...  14.9 us
  transfers between devices with their start and end apart: 13, of which 6 were waited for; matrix products, arithmetic and copies ran while one was open for 33% of the time, Pallas kernels for 4%

profile of v2, /device:TPU:0, one launch (start us, length us, event | category | flops | bytes accessed | tf_op | source)
XLA Modules:
  0.0 423.4 jit_solution(2707008581573987179)
XLA Ops:
  7.2 3.2 pad_maximum_fusion.2
  10.4 1.2 copy-done.2
  12.4 5.8 %fusion.56 = f32[512,2152]{0,1:T(8,128)S(1)} fusion(bf16[1152,2152]{0,1:T(8,128)(2,1)} %param.20, bf16[512,1152]{1,0:T(8,128)(2,1)S(1)} %copy-done.2, f32[1152]{0:T(1024)S(1)} %copy-done.10, f32[1152]{0:T(1024)S(1)} %copy-done.11, f32[512]{0:T(512)S(1)} %add_rsqrt_fusion.1, f32[512]{0:T(512)S(1)} %broadcast_multiply_fusion), kind=kOutput, calls=%fused_computation.113 | convolution fusion | flops 2542141440 | bytes 10558464 | tf_op jit(solution)/shard_map/dot_general | solution.py:20
  18.3 5.4 %fusion.60 = (bf16[512,1152]{1,0:T(8,128)(2,1)}, f32[512,1152]{1,0:T(8,128)}) fusion(bf16[2152,1152]{1,0:T(8,128)(2,1)S(1)} %bitcast.173, f32[512,2152]{0,1:T(8,128)S(1)} %fusion.56), kind=kOutput, calls=%fused_computation.116 | convolution fusion | flops 2549108736 | bytes 12904448 | tf_op jit(solution)/shard_map/dot_general | solution.py:185
  23.7 2.9 collective-permute-start
  27.0 14.9 %fusion.28 = f32[1152,2152]{1,0:T(8,128)} fusion(bf16[2152,1152]{1,0:T(8,128)(2,1)} %param.21, f32[512,2152]{0,1:T(8,128)} %copy-done.12, bf16[512,1152]{1,0:T(8,128)(2,1)} %param.33, pred[512]{0:T(512)(128)(4,1)S(1)} %broadcast_in_dim.70, bf16[512,1152]{1,0:T(8,128)(2,1)S(1)} %copy-done.2, f32[1152]{0:T(1024)S(1)} %copy-done.10, f32[1152]{0:T(1024)S(1)} %copy-done.11, ...), kind=kOutput, calls=%fused_computation.66 | convolution fusion | flops 5102268416 | bytes 21655040 | tf_op jit(solution)/shard_map/dot_general | solution.py:227
  41.9 6.1 %fusion.16 = bf16[8,72,2152]{2,1,0:T(8,128)(2,1)} fusion(f32[8,2,72,2152]{3,2,1,0:T(8,128)} %bitcast.163, pred[]{:T(512)S(6)} %eq.96), kind=kLoop, calls=%fused_computation.38 | loop fusion | flops 1239552 | bytes 7437313 | tf_op jit(solution)/shard_map/convert_element_type | solution.py:145
  48.0 7.5 %fusion.33 = f32[1152,2152]{1,0:T(8,128)} fusion(bf16[512,1152]{1,0:T(8,128)(2,1)S(1)} %copy-done.8, pred[512]{0:T(512)(128)(4,1)S(1)} %broadcast_in_dim.70, f32[512,2152]{0,1:T(8,128)S(1)} %copy-done.13), kind=kOutput, calls=%fused_computation.75 | convolution fusion | flops 2549108736 | bytes 15503872 | tf_op jit(solution)/shard_map/dot_general | solution.py:224
  58.2 6.2 %all-to-all-start = ((bf16[16,32,1152]{2,1,0:T(8,128)(2,1)}), bf16[16,32,1152]{2,1,0:T(8,128)(2,1)S(1)}, u32[]{:S(2)}, u32[]{:S(2)}) async-start(bf16[16,32,1152]{2,1,0:T(8,128)(2,1)} %bitcast.48), calls=%async_computation | async-start | bytes 2359296 | tf_op jit(solution)/shard_map/all_to_all | solution.py:201
  64.4 6.3 %fusion.15 = bf16[8,72,2152]{2,1,0:T(8,128)(2,1)} fusion(f32[8,2,72,2152]{3,2,1,0:T(8,128)} %bitcast.161, pred[]{:T(512)S(6)} %eq.96), kind=kLoop, calls=%fused_computation.37 | loop fusion | flops 1239552 | bytes 7437313 | tf_op jit(solution)/shard_map/convert_element_type | solution.py:145
  70.9 2.3 slice.71
  74.8 7.5 %fusion.3 = f32[8,72,2152]{2,1,0:T(8,128)} fusion(bf16[8,72,2152]{2,1,0:T(8,128)(2,1)} %collective-permute-done.5, f32[8,2,72,2152]{3,2,1,0:T(8,128)} %bitcast.164, pred[]{:T(512)S(6)} %eq.96), kind=kLoop, calls=%fused_computation.16 | loop fusion | flops 3718656 | bytes 17353728 | tf_op jit(solution)/shard_map/add | solution.py:147
  82.3 26.2 %all-to-all-done = bf16[16,32,1152]{2,1,0:T(8,128)(2,1)S(1)} async-done(((bf16[16,32,1152]{2,1,0:T(8,128)(2,1)}), bf16[16,32,1152]{2,1,0:T(8,128)(2,1)S(1)}, u32[]{:S(2)}, u32[]{:S(2)}) %all-to-all-start) | async-done | bytes 1179680 | tf_op jit(solution)/shard_map/all_to_all | solution.py:201
  109.9 12.1 %fusion.4 = bf16[512,4096]{1,0:T(8,128)(2,1)} fusion(bf16[512,1152]{1,0:T(8,128)(2,1)S(1)} %reshape.202, bf16[1152,4096]{1,0:T(8,128)(2,1)} %param.22, bf16[640,4096]{1,0:T(8,128)(2,1)} %param.28, f32[4096]{0:T(1024)S(1)} %copy-done.9, pred[512]{0:T(512)(128)(4,1)S(1)} %broadcast_in_dim.67), kind=kOutput, calls=%fused_computation.20 | convolution fusion | flops 4838129664 | bytes 19022336 | tf_op jit(solution)/shard_map/dot_general | solution.py:208
  122.6 2.8 fusion.23
  125.6 5.8 %bitcast_add_fusion = f32[8,72,2152]{2,1,0:T(8,128)S(1)} fusion(bf16[8,72,2152]{2,1,0:T(8,128)(2,1)} %collective-permute-done.3, f32[8,2,72,2152]{3,2,1,0:T(8,128)} %bitcast.162, pred[]{:T(512)S(6)} %eq.96), kind=kLoop, calls=%fused_computation.17 | loop fusion | flops 3718656 | bytes 17353728 | tf_op jit(solution)/shard_map/add | solution.py:147
  131.6 1.9 collective-permute-start.4
  133.5 1.2 fusion.36
  135.0 47.8 %collective-permute-done.6 = bf16[4,72,2152]{2,1,0:T(8,128)(2,1)S(1)} collective-permute-done((bf16[4,72,2152]{2,1,0:T(8,128)(2,1)S(1)}, bf16[4,72,2152]{2,1,0:T(8,128)(2,1)S(1)}, u32[]{:S(2)}, u32[]{:S(2)}) %collective-permute-start.6) | collective-permute-done | bytes 1239584 | tf_op jit(solution)/shard_map/ppermute | solution.py:146
  183.1 52.8 %collective-permute-done.4 = bf16[4,72,2152]{2,1,0:T(8,128)(2,1)S(1)} collective-permute-done((bf16[4,72,2152]{2,1,0:T(8,128)(2,1)S(1)}, bf16[4,72,2152]{2,1,0:T(8,128)(2,1)S(1)}, u32[]{:S(2)}, u32[]{:S(2)}) %collective-permute-start.4) | collective-permute-done | bytes 1239584 | tf_op jit(solution)/shard_map/ppermute | solution.py:146
  235.9 1.8 bitcast_add_fusion.2
  238.3 1.3 constant_dynamic-update-slice_fusion
  239.6 5.0 %broadcast_select_fusion.1 = (bf16[640,4096]{1,0:T(8,128)(2,1)S(1)}, bf16[640,4096]{1,0:T(8,128)(2,1)S(1)}) fusion(bf16[640,4096]{1,0:T(8,128)(2,1)S(1)} %constant_dynamic-update-slice_fusion, pred[]{:T(512)S(6)} %eq.85, bf16[128,4096]{1,0:T(8,128)(2,1)} %slice.71, bf16[512,4096]{1,0:T(8,128)(2,1)} %fusion.4), kind=kLoop, calls=%fused_computation.12 | loop fusion | flops 15728640 | bytes 20971520 | tf_op jit(solution)/shard_map/jit(_where)/select_n | solution.py:132
  244.6 6.0 %fusion.1 = (f32[640]{0:T(1024)S(1)}, bf16[640,8192]{1,0:T(8,128)(2,1)}) fusion(bf16[640,4096]{1,0:T(8,128)(2,1)S(1)} %get-tuple-element.18, bf16[640,4096]{1,0:T(8,128)(2,1)S(1)} %get-tuple-element.17, f32[8192]{0:T(1024)S(1)} %copy-done.4), kind=kLoop, calls=%fused_computation.5 | loop fusion | flops 41942400 | bytes 21006848 | tf_op jit(solution)/shard_map/reduce_sum | solution.py:214
  250.6 75.6 %all-gather.2.cloned.1.call-done = bf16[8192,3072]{1,0:T(8,128)(2,1)} async-done(((bf16[512,3072]{1,0:T(8,128)(2,1)}), bf16[8192,3072]{1,0:T(8,128)(2,1)}) %all-gather.2.cloned.1.call-update) | async-done | bytes 50331664 | tf_op jit(solution)/shard_map/all_gather | solution.py:176
  326.2 1.8 fusion.30
  328.2 2.1 collective-permute-start.7
  330.3 38.7 %fusion.61.q_ref.k_ref.v_ref = f32[640,3072]{1,0:T(8,128)S(1)} fusion(bf16[640,8192]{1,0:T(8,128)(2,1)} %get-tuple-element.8, bf16[8192,3072]{1,0:T(8,128)(2,1)} %all-gather.2.cloned.1.call-done), kind=kOutput, calls=%fused_computation.117 | convolution fusion | flops 32212254720 | bytes 68681728 | tf_op jit(solution)/shard_map/dot_general | solution.py:238
  369.2 15.8 %shard_map.184 = bf16[640,2048]{1,0:T(8,128)(2,1)} custom-call(f32[640,3072]{1,0:T(8,128)S(1)} %fusion.61.q_ref.k_ref.v_ref, f32[640,3072]{1,0:T(8,128)S(1)} %fusion.61.q_ref.k_ref.v_ref, f32[640,3072]{1,0:T(8,128)S(1)} %fusion.61.q_ref.k_ref.v_ref, f32[640,1]{1,0:T(8,128)S(1)} %broadcast_in_dim.76.inv_ref, f32[640,128]{1,0:T(8,128)S(1)} %get-tuple-element.25.cos_ref, ...), custom_call_target="tpu_custom_call" | custom-call | flops 3355443200 | bytes 7864320 | tf_op jit(solution)/shard_map/pallas_call | solution.py:89
  385.2 2.5 collective-permute-start.10
  388.6 21.3 %collective-permute-done.10 = bf16[1,72,2152]{2,1,0:T(8,128)(2,1)S(1)} collective-permute-done((bf16[1,72,2152]{2,1,0:T(8,128)(2,1)S(1)}, bf16[1,72,2152]{2,1,0:T(8,128)(2,1)S(1)}, u32[]{:S(2)}, u32[]{:S(2)}) %collective-permute-start.10) | collective-permute-done | bytes 309920 | tf_op jit(solution)/shard_map/ppermute | solution.py:146
  410.8 4.6 %collective-permute-done.8 = bf16[1,72,2152]{2,1,0:T(8,128)(2,1)S(1)} collective-permute-done((bf16[1,72,2152]{2,1,0:T(8,128)(2,1)S(1)}, bf16[1,72,2152]{2,1,0:T(8,128)(2,1)S(1)}, u32[]{:S(2)}, u32[]{:S(2)}) %collective-permute-start.8) | collective-permute-done | bytes 309920 | tf_op jit(solution)/shard_map/ppermute | solution.py:146
  (93 shorter events, 12.2 us)
Async XLA Ops:
  7.2 319.0 %all-gather.2.cloned.1.call-start = ((), (), s32[]{:S(2)}) async-start(), calls=%async_computation.1 | async-start | bytes 53477376 | tf_op jit(solution)/shard_map/all_gather | solution.py:176
  10.4 1.3 copy-start.2
  10.4 2.0 copy-start.10
  10.4 2.0 copy-start.11
  11.9 6.3 %slice-start.2 = ((s8[4958208]{0:T(1024)(128)(4,1)}), s8[4194304]{0:T(1024)(128)(4,1)S(1)}, s32[]{:S(2)}) async-start(s8[4958208]{0:T(1024)(128)(4,1)} %bitcast.172), calls=%async_computation.4 | async-start | bytes 8388608
  12.4 5.9 %slice-start.3 = ((s8[4958208]{0:T(1024)(128)(4,1)}), s8[763904]{0:T(1024)(128)(4,1)S(1)}, s32[]{:S(2)}) async-start(s8[4958208]{0:T(1024)(128)(4,1)} %bitcast.172), calls=%async_computation.5 | async-start | bytes 1527808
  18.3 5.4 %copy-start.12 = (f32[512,2152]{0,1:T(8,128)}, f32[512,2152]{0,1:T(8,128)S(1)}, u32[]{:S(2)}) copy-start(f32[512,2152]{0,1:T(8,128)S(1)} %fusion.56) | copy-start | bytes 13221892
  18.3 8.4 %copy-start.7 = (s32[16,2]{0,1:T(2,128)S(1)}, s32[16,2]{0,1:T(2,128)}, u32[]{:S(2)}) copy-start(s32[16,2]{0,1:T(2,128)} %param.24) | copy-start | bytes 388
  18.3 8.4 %copy-start.5 = (s32[16,16]{1,0:T(8,128)S(1)}, s32[16,16]{1,0:T(8,128)}, u32[]{:S(2)}) copy-start(s32[16,16]{1,0:T(8,128)} %param.25) | copy-start | bytes 3076
  23.7 31.9 %collective-permute-start = (bf16[512,1152]{1,0:T(8,128)(2,1)}, bf16[512,1152]{1,0:T(8,128)(2,1)S(1)}, u32[]{:S(2)}, u32[]{:S(2)}) collective-permute-start(bf16[512,1152]{1,0:T(8,128)(2,1)} %get-tuple-element.23), channel_id=1, source_target_pairs={{0,1},{1,0},{2,3},{3,2},{4,5},{5,4},{6,7},{7,6},{8,9},{9,8},{10,11... | collective-permute-start | bytes 3538952 | tf_op jit(solution)/shard_map/ppermute | solution.py:116
  41.9 6.1 %copy-start.8 = (bf16[512,1152]{1,0:T(8,128)(2,1)S(1)}, bf16[512,1152]{1,0:T(8,128)(2,1)}, u32[]{:S(2)}) copy-start(bf16[512,1152]{1,0:T(8,128)(2,1)} %param.33) | copy-start | bytes 3538948
  41.9 6.1 %copy-start.13 = (f32[512,2152]{0,1:T(8,128)S(1)}, f32[512,2152]{0,1:T(8,128)}, u32[]{:S(2)}) copy-start(f32[512,2152]{0,1:T(8,128)} %copy-done.12) | copy-start | bytes 13221892
  48.0 26.9 %collective-permute-start.5 = (bf16[8,72,2152]{2,1,0:T(8,128)(2,1)}, bf16[8,72,2152]{2,1,0:T(8,128)(2,1)}, u32[]{:S(2)}, u32[]{:S(2)}) collective-permute-start(bf16[8,72,2152]{2,1,0:T(8,128)(2,1)} %fusion.16), channel_id=1, source_target_pairs={{0,2},{2,0},{4,6},{6,4},{8,10},{10,8},{12,14},{14,12},{16,18},{18,... | collective-permute-start | bytes 7437320 | tf_op jit(solution)/shard_map/ppermute | solution.py:146
  48.0 7.6 %copy-start.3 = (f32[512,1152]{1,0:T(8,128)S(1)}, f32[512,1152]{1,0:T(8,128)}, u32[]{:S(2)}) copy-start(f32[512,1152]{1,0:T(8,128)} %get-tuple-element.24) | copy-start | bytes 7077892
  58.2 50.3 %all-to-all-start = ((bf16[16,32,1152]{2,1,0:T(8,128)(2,1)}), bf16[16,32,1152]{2,1,0:T(8,128)(2,1)S(1)}, u32[]{:S(2)}, u32[]{:S(2)}) async-start(bf16[16,32,1152]{2,1,0:T(8,128)(2,1)} %bitcast.48), calls=%async_computation | async-start | bytes 2359296 | tf_op jit(solution)/shard_map/all_to_all | solution.py:201
  64.4 9.4 %copy-start.6 = (s32[16,16]{1,0:T(8,128)S(1)}, s32[16,16]{1,0:T(8,128)}, u32[]{:S(2)}) copy-start(s32[16,16]{1,0:T(8,128)} %param.26) | copy-start | bytes 3076
  64.4 9.8 %copy-start = (s32[1,640]{1,0:T(1,128)S(1)}, s32[1,640]{1,0:T(1,128)}, u32[]{:S(2)}) copy-start(s32[1,640]{1,0:T(1,128)} %col_ref.1) | copy-start | bytes 7684
  70.7 54.8 %collective-permute-start.3 = (bf16[8,72,2152]{2,1,0:T(8,128)(2,1)}, bf16[8,72,2152]{2,1,0:T(8,128)(2,1)}, u32[]{:S(2)}, u32[]{:S(2)}) collective-permute-start(bf16[8,72,2152]{2,1,0:T(8,128)(2,1)} %fusion.15), channel_id=1, source_target_pairs={{0,2},{2,0},{4,6},{6,4},{8,10},{10,8},{12,14},{14,12},{16,18},{18,... | collective-permute-start | bytes 7437320 | tf_op jit(solution)/shard_map/ppermute | solution.py:146
  73.2 165.1 %collective-permute-start.2 = (bf16[128,4096]{1,0:T(8,128)(2,1)}, bf16[128,4096]{1,0:T(8,128)(2,1)}, u32[]{:S(2)}, u32[]{:S(2)}) collective-permute-start(bf16[128,4096]{1,0:T(8,128)(2,1)} %slice.71), channel_id=1, source_target_pairs={{0,1},{1,0},{2,3},{3,2},{4,5},{5,4},{6,7},{7,6},{8,9},{9,8},{10,11... | collective-permute-start | bytes 3145736 | tf_op jit(solution)/shard_map/ppermute | solution.py:116
  108.5 1.4 copy-start.9
  122.0 115.8 %collective-permute-start.1 = (bf16[512,4096]{1,0:T(8,128)(2,1)}, bf16[512,4096]{1,0:T(8,128)(2,1)S(1)}, u32[]{:S(2)}, u32[]{:S(2)}) collective-permute-start(bf16[512,4096]{1,0:T(8,128)(2,1)} %fusion.4), channel_id=1, source_target_pairs={{0,1},{1,0},{2,3},{3,2},{4,5},{5,4},{6,7},{7,6},{8,9},{9,8},{10,11... | collective-permute-start | bytes 12582920 | tf_op jit(solution)/shard_map/ppermute | solution.py:116
  122.6 60.2 %slice-start = ((s8[5013504]{0:T(1024)(128)(4,1)}), s8[4194304]{0:T(1024)(128)(4,1)S(1)}, s32[]{:S(2)}) async-start(s8[5013504]{0:T(1024)(128)(4,1)} %bitcast.156), calls=%async_computation.2 | async-start | bytes 8388608
  125.5 57.3 %slice-start.1 = ((s8[5013504]{0:T(1024)(128)(4,1)}), s8[819200]{0:T(1024)(128)(4,1)S(1)}, s32[]{:S(2)}) async-start(s8[5013504]{0:T(1024)(128)(4,1)} %bitcast.156), calls=%async_computation.3 | async-start | bytes 1638400
  125.5 57.3 %collective-permute-start.6 = (bf16[4,72,2152]{2,1,0:T(8,128)(2,1)S(1)}, bf16[4,72,2152]{2,1,0:T(8,128)(2,1)S(1)}, u32[]{:S(2)}, u32[]{:S(2)}) collective-permute-start(bf16[4,72,2152]{2,1,0:T(8,128)(2,1)S(1)} %fusion.23), channel_id=1, source_target_pairs={{0,4},{2,6},{4,0},{6,2},{8,12},{10,14},{12,8},{14,10},{16,20},{18,... | collective-permute-start | bytes 3718664 | tf_op jit(solution)/shard_map/ppermute | solution.py:146
  131.6 104.4 %collective-permute-start.4 = (bf16[4,72,2152]{2,1,0:T(8,128)(2,1)S(1)}, bf16[4,72,2152]{2,1,0:T(8,128)(2,1)S(1)}, u32[]{:S(2)}, u32[]{:S(2)}) collective-permute-start(bf16[4,72,2152]{2,1,0:T(8,128)(2,1)S(1)} %fusion.22), channel_id=1, source_target_pairs={{0,4},{2,6},{4,0},{6,2},{8,12},{10,14},{12,8},{14,10},{16,20},{18,... | collective-permute-start | bytes 3718664 | tf_op jit(solution)/shard_map/ppermute | solution.py:146
  239.6 5.0 %copy-start.4 = (f32[8192]{0:T(1024)S(1)}, f32[8192]{0:T(1024)}, u32[]{:S(2)}) copy-start(f32[8192]{0:T(1024)} %param.29) | copy-start | bytes 98308
  328.0 56.9 %collective-permute-start.9 = (bf16[2,72,2152]{2,1,0:T(8,128)(2,1)S(1)}, bf16[2,72,2152]{2,1,0:T(8,128)(2,1)S(1)}, u32[]{:S(2)}, u32[]{:S(2)}) collective-permute-start(bf16[2,72,2152]{2,1,0:T(8,128)(2,1)S(1)} %fusion.30), channel_id=1, source_target_pairs={{0,8},{2,10},{4,12},{6,14},{8,0},{10,2},{12,4},{14,6},{16,24},{18,... | collective-permute-start | bytes 1859336 | tf_op jit(solution)/shard_map/ppermute | solution.py:146
  328.2 59.5 %collective-permute-start.7 = (bf16[2,72,2152]{2,1,0:T(8,128)(2,1)S(1)}, bf16[2,72,2152]{2,1,0:T(8,128)(2,1)S(1)}, u32[]{:S(2)}, u32[]{:S(2)}) collective-permute-start(bf16[2,72,2152]{2,1,0:T(8,128)(2,1)S(1)} %fusion.29), channel_id=1, source_target_pairs={{0,8},{2,10},{4,12},{6,14},{8,0},{10,2},{12,4},{14,6},{16,24},{18,... | collective-permute-start | bytes 1859336 | tf_op jit(solution)/shard_map/ppermute | solution.py:146
  369.1 15.8 %copy-start.1 = (f32[4,72,2152]{2,1,0:T(8,128)S(1)}, f32[4,72,2152]{2,1,0:T(8,128)}, u32[]{:S(2)}) copy-start(f32[4,72,2152]{2,1,0:T(8,128)} %bitcast_add_fusion.2) | copy-start | bytes 7437316
  385.2 24.7 %collective-permute-start.10 = (bf16[1,72,2152]{2,1,0:T(8,128)(2,1)S(1)}, bf16[1,72,2152]{2,1,0:T(8,128)(2,1)S(1)}, u32[]{:S(2)}, u32[]{:S(2)}) collective-permute-start(bf16[1,72,2152]{2,1,0:T(8,128)(2,1)S(1)} %fusion.35), channel_id=1, source_target_pairs={{0,16},{2,18},{4,20},{6,22},{8,24},{10,26},{12,28},{14,30},{16,0},... | collective-permute-start | bytes 929672 | tf_op jit(solution)/shard_map/ppermute | solution.py:146
  388.0 27.4 %collective-permute-start.8 = (bf16[1,72,2152]{2,1,0:T(8,128)(2,1)S(1)}, bf16[1,72,2152]{2,1,0:T(8,128)(2,1)S(1)}, u32[]{:S(2)}, u32[]{:S(2)}) collective-permute-start(bf16[1,72,2152]{2,1,0:T(8,128)(2,1)S(1)} %fusion.34), channel_id=1, source_target_pairs={{0,16},{2,18},{4,20},{6,22},{8,24},{10,26},{12,28},{14,30},{16,0},... | collective-permute-start | bytes 929672 | tf_op jit(solution)/shard_map/ppermute | solution.py:146
Sparse Core Ops, SparseCore 0:
  10.5 315.6 all-gather.1

commit v3 on v1

--- a/solution.py
+++ b/solution.py
@@ -79,20 +79,19 @@
         )
 
 
-def attend(raw, q_cols, kv_cols, inverse, positions, segments):
-    count = raw.shape[0]
+def attend(raw_q, raw_kv, q_cols, kv_cols, inverse, positions, segments):
+    count = raw_q.shape[0]
     groups = kv_cols // HEAD
     wide = q_cols // groups
     cosine, sine = rope_tables(positions)
-    q_blocks = q_cols // HEAD
     whole = lambda g: (0, 0)
     return pl.pallas_call(
         attention_kernel,
         grid=(groups,),
         in_specs=[
             pl.BlockSpec((count, wide), lambda g: (0, g)),
-            pl.BlockSpec((count, HEAD), lambda g: (0, q_blocks + g)),
-            pl.BlockSpec((count, HEAD), lambda g: (0, q_blocks + groups + g)),
+            pl.BlockSpec((count, HEAD), lambda g: (0, g)),
+            pl.BlockSpec((count, HEAD), lambda g: (0, groups + g)),
             pl.BlockSpec((count, 1), whole),
             pl.BlockSpec((count, HEAD), whole),
             pl.BlockSpec((count, HEAD), whole),
@@ -108,7 +107,7 @@
             transcendentals=count * count * (q_cols // HEAD),
         ),
     )(
-        raw, raw, raw, inverse[:, None], cosine, sine, segments[:, None], segments[None, :]
+        raw_q, raw_kv, raw_kv, inverse[:, None], cosine, sine, segments[:, None], segments[None, :]
     )
 
 
@@ -175,8 +174,9 @@
     slot_count = tile_owner.shape[1]
     tile_rows = TILE_ROWS
     enc_rows = tiles.shape[0]
-    full_weights = lax.all_gather(
-        jnp.concatenate([q_weight, k_weight, v_weight], axis=1), "dp", axis=0, tiled=True
+    full_q = lax.all_gather(q_weight, "dp", axis=0, tiled=True)
+    full_kv = lax.all_gather(
+        jnp.concatenate([k_weight, v_weight], axis=1), "dp", axis=0, tiled=True
     )
     totals = jnp.sum(tile_counts, axis=1)
     slot_ids = jnp.arange(slot_count, dtype=jnp.int32)
@@ -218,8 +218,9 @@
     segments = segment_ids[0]
     positions = segment_positions(segments)
     scaled, inverse = lax.optimization_barrier((scaled, inverse))
-    raw = jnp.dot(scaled, full_weights, preferred_element_type=jnp.float32)
-    context = attend(raw, q_weight.shape[1], k_weight.shape[1], inverse, positions, segments)
+    raw_q = jnp.dot(scaled, full_q, preferred_element_type=jnp.float32)
+    raw_kv = jnp.dot(scaled, full_kv, preferred_element_type=jnp.float32)
+    context = attend(raw_q, raw_kv, q_weight.shape[1], k_weight.shape[1], inverse, positions, segments)
     live_rows = jnp.repeat(my_live, tile_rows)[:, None]
     cotangent = jnp.where(live_rows, feature_grad, jnp.zeros_like(feature_grad))
     hidden_grad = lax.dot_general(

time: 391 us -> 424 us (1.084)
  waiting for transfers between devices: 191 us -> 203 us
  starting transfers between devices: 21.2 us -> 32.7 us
  matrix products: 80.9 us -> 89.4 us
  other arithmetic: 48.4 us -> 52.9 us
    all_gather x1 -> x2, waiting for transfers between devices: 22.5 us -> 77.5 us  [the longest x1 77.5 us: body(): full_q = lax.all_gather(q_weight, 'dp', axis=0, tiled=True)]
    ppermute x8, waiting for transfers between devices: 121 us -> 79.4 us  [sum_scatter(): arrived = lax.ppermute(other, 'dp', [(i, i ^ step) for i in range(size)])]
    ppermute x8, starting transfers between devices: 9.36 us -> 21.3 us  [sum_scatter(): arrived = lax.ppermute(other, 'dp', [(i, i ^ step) for i in range(size)])]
    convert_element_type x8, other arithmetic: 11 us -> 17.3 us  [sum_scatter(): other = jnp.where(bit == 0, pairs[:, 1], pairs[:, 0]).astype(jnp.bfloat16)]
    dot_general x1 -> x2, matrix products: 38.8 us -> 43.2 us  [the longest x1 26.6 us: body(): raw_q = jnp.dot(scaled, full_q, preferred_element_type=jnp.float32)]
    unnamed x37 -> x45, local copies, waits for them, and re-layouts: 9.96 us -> 5.68 us
  transfers between devices with their start and end apart: 13 -> 14, of which waited for: 8 -> 8; matrix products, arithmetic and copies ran while one was open for 25% -> 29% of each run, Pallas kernels for 0% -> 0%
where the time goes in v3:
time: 424 us; the launch traced here: 421 us
  waiting for transfers between devices  203 us (48%)
  matrix products  89.4 us (21%)
  other arithmetic  52.9 us (12%)
  starting transfers between devices  32.7 us (8%)
  Pallas kernels  15.6 us (4%)
  between operations  14.7 us (3%)
  local copies, waits for them, and re-layouts  12.7 us (3%)
    ppermute x8, waiting for transfers between devices, sum_scatter(): arrived = lax.ppermute(other, 'dp', [(i, i ^ step) for i in range(size)])  79.4 us
    all_gather x1, waiting for transfers between devices, body(): full_q = lax.all_gather(q_weight, 'dp', axis=0, tiled=True)  77.5 us
    dot_general x1, matrix products, body(): raw_q = jnp.dot(scaled, full_q, preferred_element_type=jnp.float32)  26.6 us
    all_to_all x1, waiting for transfers between devices, body(): lax.all_to_all(outbound, 'dp', split_axis=0, concat_axis=0, tiled=True)  23.7 us
    ppermute x3, waiting for transfers between devices, swap_mp(): return lax.ppermute(values, 'mp', [(0, 1), (1, 0)])  21.5 us
    ppermute x8, starting transfers between devices, sum_scatter(): arrived = lax.ppermute(other, 'dp', [(i, i ^ step) for i in range(size)])  21.3 us
    convert_element_type x8, other arithmetic, sum_scatter(): other = jnp.where(bit == 0, pairs[:, 1], pairs[:, 0]).astype(jnp.bfloat16)  17.3 us
    dot_general x1, matrix products, body(): raw_kv = jnp.dot(scaled, full_kv, preferred_element_type=jnp.float32)  16.6 us
  transfers between devices with their start and end apart: 14, of which 8 were waited for; matrix products, arithmetic and copies ran while one was open for 29% of the time, Pallas kernels for 0%

profile of v3, /device:TPU:0, one launch (start us, length us, event | category | flops | bytes accessed | tf_op | source)
XLA Modules:
  0.0 420.9 jit_solution(6895693409446248107)
XLA Ops:
  7.2 2.4 pad_maximum_fusion.2
  11.6 6.0 %fusion.56 = f32[512,2152]{0,1:T(8,128)S(1)} fusion(bf16[1152,2152]{0,1:T(8,128)(2,1)} %param.20, bf16[512,1152]{1,0:T(8,128)(2,1)S(1)} %copy-done.4, f32[1152]{0:T(1024)S(1)} %copy-done.12, f32[1152]{0:T(1024)S(1)} %copy-done.13, f32[512]{0:T(512)S(1)} %add_rsqrt_fusion.1, f32[512]{0:T(512)S(1)} %broadcast_multiply_fusion), kind=kOutput, calls=%fused_computation.113 | convolution fusion | flops 2542141440 | bytes 10558464 | tf_op jit(solution)/shard_map/dot_general | solution.py:20
  17.6 7.2 %fusion.33 = f32[1152,2152]{1,0:T(8,128)} fusion(bf16[512,1152]{1,0:T(8,128)(2,1)S(1)} %copy-done.10, pred[512]{0:T(512)(128)(4,1)S(1)} %broadcast_in_dim.73, f32[512,2152]{0,1:T(8,128)S(1)} %fusion.56), kind=kOutput, calls=%fused_computation.75 | convolution fusion | flops 2549108736 | bytes 15503872 | tf_op jit(solution)/shard_map/dot_general | solution.py:230
  24.8 5.9 %fusion.16 = bf16[8,72,2152]{2,1,0:T(8,128)(2,1)} fusion(f32[8,2,72,2152]{3,2,1,0:T(8,128)} %bitcast.20, pred[]{:T(512)S(6)} %eq.102), kind=kLoop, calls=%fused_computation.37 | loop fusion | flops 1239552 | bytes 7437313 | tf_op jit(solution)/shard_map/convert_element_type | solution.py:146
  31.2 14.9 %fusion.28 = f32[1152,2152]{1,0:T(8,128)} fusion(bf16[2152,1152]{1,0:T(8,128)(2,1)} %param.21, f32[512,2152]{0,1:T(8,128)} %copy-done.14, bf16[512,1152]{1,0:T(8,128)(2,1)} %param.33, pred[512]{0:T(512)(128)(4,1)S(1)} %broadcast_in_dim.73, bf16[512,1152]{1,0:T(8,128)(2,1)S(1)} %copy-done.4, f32[1152]{0:T(1024)S(1)} %copy-done.12, f32[1152]{0:T(1024)S(1)} %copy-done.13, ...), kind=kOutput, calls=%fused_computation.65 | convolution fusion | flops 5102268416 | bytes 21655040 | tf_op jit(solution)/shard_map/dot_general | solution.py:233
  46.1 6.0 %fusion.15 = bf16[8,72,2152]{2,1,0:T(8,128)(2,1)} fusion(f32[8,2,72,2152]{3,2,1,0:T(8,128)} %bitcast.161, pred[]{:T(512)S(6)} %eq.102), kind=kLoop, calls=%fused_computation.36 | loop fusion | flops 1239552 | bytes 7437313 | tf_op jit(solution)/shard_map/convert_element_type | solution.py:146
  52.2 7.9 %fusion.60 = (bf16[512,1152]{1,0:T(8,128)(2,1)}, f32[512,1152]{1,0:T(8,128)}) fusion(bf16[2152,1152]{1,0:T(8,128)(2,1)} %param.21, f32[512,2152]{0,1:T(8,128)S(1)} %copy-done.15), kind=kOutput, calls=%fused_computation.116 | convolution fusion | flops 2549108736 | bytes 12904448 | tf_op jit(solution)/shard_map/dot_general | solution.py:187
  60.0 2.9 collective-permute-start
  63.0 2.3 slice.71
  68.5 21.5 %collective-permute-done = bf16[512,1152]{1,0:T(8,128)(2,1)} collective-permute-done((bf16[512,1152]{1,0:T(8,128)(2,1)}, bf16[512,1152]{1,0:T(8,128)(2,1)}, u32[]{:S(2)}, u32[]{:S(2)}) %collective-permute-start) | collective-permute-done | bytes 1179680 | tf_op jit(solution)/shard_map/ppermute | solution.py:115
  94.0 6.9 %all-to-all-start = ((bf16[16,32,1152]{2,1,0:T(8,128)(2,1)}), bf16[16,32,1152]{2,1,0:T(8,128)(2,1)}, u32[]{:S(2)}, u32[]{:S(2)}) async-start(bf16[16,32,1152]{2,1,0:T(8,128)(2,1)} %bitcast.169), calls=%async_computation | async-start | bytes 2359296 | tf_op jit(solution)/shard_map/all_to_all | solution.py:203
  100.9 7.9 %fusion.3 = f32[8,72,2152]{2,1,0:T(8,128)} fusion(bf16[8,72,2152]{2,1,0:T(8,128)(2,1)} %collective-permute-done.7, f32[8,2,72,2152]{3,2,1,0:T(8,128)} %bitcast.20, pred[]{:T(512)S(6)} %eq.102), kind=kLoop, calls=%fused_computation.16 | loop fusion | flops 3718656 | bytes 17353728 | tf_op jit(solution)/shard_map/add | solution.py:148
  108.8 3.8 fusion.23
  112.6 1.9 collective-permute-start.8
  114.6 2.3 bitcast_add_fusion
  116.9 2.3 copy-done.3
  120.6 23.7 %all-to-all-done = bf16[16,32,1152]{2,1,0:T(8,128)(2,1)} async-done(((bf16[16,32,1152]{2,1,0:T(8,128)(2,1)}), bf16[16,32,1152]{2,1,0:T(8,128)(2,1)}, u32[]{:S(2)}, u32[]{:S(2)}) %all-to-all-start) | async-done | bytes 1179680 | tf_op jit(solution)/shard_map/all_to_all | solution.py:203
  147.8 9.3 %fusion.4 = bf16[512,4096]{1,0:T(8,128)(2,1)S(1)} fusion(bf16[512,1152]{1,0:T(8,128)(2,1)} %reshape.208, bf16[1152,4096]{1,0:T(8,128)(2,1)} %param.22, bf16[640,4096]{1,0:T(8,128)(2,1)} %param.28, f32[4096]{0:T(1024)S(1)} %copy-done.11, pred[512]{0:T(512)(128)(4,1)S(1)} %broadcast_in_dim.67), kind=kOutput, calls=%fused_computation.20 | convolution fusion | flops 4838129664 | bytes 19022336 | tf_op jit(solution)/shard_map/dot_general | solution.py:210
  158.6 3.2 bitcast_add_fusion.1
  161.9 13.1 %collective-permute-start.9 = (bf16[2,72,2152]{2,1,0:T(8,128)(2,1)S(1)}, bf16[2,72,2152]{2,1,0:T(8,128)(2,1)S(1)}, u32[]{:S(2)}, u32[]{:S(2)}) collective-permute-start(bf16[2,72,2152]{2,1,0:T(8,128)(2,1)S(1)} %fusion.30), channel_id=1, source_target_pairs={{0,8},{2,10},{4,12},{6,14},{8,0},{10,2},{12,4},{14,6},{16,24},{18,... | collective-permute-start | bytes 1859336 | tf_op jit(solution)/shard_map/ppermute | solution.py:147
  175.0 8.3 %collective-permute-done.4 = bf16[4,72,2152]{2,1,0:T(8,128)(2,1)} collective-permute-done((bf16[4,72,2152]{2,1,0:T(8,128)(2,1)}, bf16[4,72,2152]{2,1,0:T(8,128)(2,1)}, u32[]{:S(2)}, u32[]{:S(2)}) %collective-permute-start.4) | collective-permute-done | bytes 1239584 | tf_op jit(solution)/shard_map/ppermute | solution.py:147
  185.3 18.1 %collective-permute-done.9 = bf16[2,72,2152]{2,1,0:T(8,128)(2,1)S(1)} collective-permute-done((bf16[2,72,2152]{2,1,0:T(8,128)(2,1)S(1)}, bf16[2,72,2152]{2,1,0:T(8,128)(2,1)S(1)}, u32[]{:S(2)}, u32[]{:S(2)}) %collective-permute-start.9) | collective-permute-done | bytes 619808 | tf_op jit(solution)/shard_map/ppermute | solution.py:147
  203.6 3.9 collective-permute-start.10
  207.5 28.9 %collective-permute-done.5 = bf16[2,72,2152]{2,1,0:T(8,128)(2,1)S(1)} collective-permute-done((bf16[2,72,2152]{2,1,0:T(8,128)(2,1)S(1)}, bf16[2,72,2152]{2,1,0:T(8,128)(2,1)S(1)}, u32[]{:S(2)}, u32[]{:S(2)}) %collective-permute-start.5) | collective-permute-done | bytes 619808 | tf_op jit(solution)/shard_map/ppermute | solution.py:147
  238.3 4.9 %collective-permute-done.10 = bf16[1,72,2152]{2,1,0:T(8,128)(2,1)S(1)} collective-permute-done((bf16[1,72,2152]{2,1,0:T(8,128)(2,1)S(1)}, bf16[1,72,2152]{2,1,0:T(8,128)(2,1)S(1)}, u32[]{:S(2)}, u32[]{:S(2)}) %collective-permute-start.10) | collective-permute-done | bytes 309920 | tf_op jit(solution)/shard_map/ppermute | solution.py:147
  244.2 19.1 %collective-permute-done.6 = bf16[1,72,2152]{2,1,0:T(8,128)(2,1)S(1)} collective-permute-done((bf16[1,72,2152]{2,1,0:T(8,128)(2,1)S(1)}, bf16[1,72,2152]{2,1,0:T(8,128)(2,1)S(1)}, u32[]{:S(2)}, u32[]{:S(2)}) %collective-permute-start.6) | collective-permute-done | bytes 309920 | tf_op jit(solution)/shard_map/ppermute | solution.py:147
  266.0 4.6 %broadcast_select_fusion.1 = (bf16[640,4096]{1,0:T(8,128)(2,1)S(1)}, bf16[640,4096]{1,0:T(8,128)(2,1)S(1)}) fusion(bf16[640,4096]{1,0:T(8,128)(2,1)S(1)} %constant_dynamic-update-slice_fusion, pred[]{:T(512)S(6)} %eq.85, bf16[128,4096]{1,0:T(8,128)(2,1)} %slice.71, bf16[512,4096]{1,0:T(8,128)(2,1)S(1)} %fusion.4), kind=kLoop, calls=%fused_computation.12 | loop fusion | flops 15728640 | bytes 20971520 | tf_op jit(solution)/shard_map/jit(_where)/select_n | solution.py:131
  270.6 5.9 %fusion.1 = (f32[640]{0:T(1024)S(1)}, bf16[640,8192]{1,0:T(8,128)(2,1)}) fusion(bf16[640,4096]{1,0:T(8,128)(2,1)S(1)} %get-tuple-element.12, bf16[640,4096]{1,0:T(8,128)(2,1)S(1)} %get-tuple-element.11, f32[8192]{0:T(1024)S(1)} %copy-done.6), kind=kLoop, calls=%fused_computation.5 | loop fusion | flops 41942400 | bytes 21006848 | tf_op jit(solution)/shard_map/reduce_sum | solution.py:216
  277.4 16.6 %fusion.62.k_ref.v_ref = f32[640,1024]{1,0:T(8,128)S(1)} fusion(bf16[640,8192]{1,0:T(8,128)(2,1)} %get-tuple-element.5, bf16[8192,1024]{1,0:T(8,128)(2,1)} %all-gather.5.cloned.1.call-done), kind=kOutput, calls=%fused_computation.118 | convolution fusion | flops 10737418240 | bytes 29884416 | tf_op jit(solution)/shard_map/dot_general | solution.py:222
  294.0 77.5 %all-gather.3.cloned.1.call-done = bf16[8192,2048]{1,0:T(8,128)(2,1)} async-done(((bf16[512,2048]{1,0:T(8,128)(2,1)}), bf16[8192,2048]{1,0:T(8,128)(2,1)}) %all-gather.3.cloned.1.call-update) | async-done | bytes 33554448 | tf_op jit(solution)/shard_map/all_gather | solution.py:177
  371.6 26.6 %fusion.61.q_ref = f32[640,2048]{1,0:T(8,128)S(1)} fusion(bf16[640,8192]{1,0:T(8,128)(2,1)} %get-tuple-element.5, bf16[8192,2048]{1,0:T(8,128)(2,1)} %all-gather.3.cloned.1.call-done), kind=kOutput, calls=%fused_computation.117 | convolution fusion | flops 21474836480 | bytes 49283072 | tf_op jit(solution)/shard_map/dot_general | solution.py:221
  398.2 15.6 %shard_map.184 = bf16[640,2048]{1,0:T(8,128)(2,1)} custom-call(f32[640,2048]{1,0:T(8,128)S(1)} %fusion.61.q_ref, f32[640,1024]{1,0:T(8,128)S(1)} %fusion.62.k_ref.v_ref, f32[640,1024]{1,0:T(8,128)S(1)} %fusion.62.k_ref.v_ref, f32[640,1]{1,0:T(8,128)S(1)} %copy-done.1, f32[640,128]{1,0:T(8,128)S(1)} %get-tuple-element.19.cos_ref, f32[640,128]{1,0:T(8,128)S(1)} %copy-done, ...), custom_call_target="tpu_custom_call" | custom-call | flops 3355443200 | bytes 7864320 | tf_op jit(solution)/shard_map/pallas_call | solution.py:88
  (103 shorter events, 24.7 us)
Async XLA Ops:
  7.2 3.3 copy-start.9
  7.2 3.3 copy-start.7
  7.2 3.7 copy-start.4
  7.2 270.2 %all-gather.5.cloned.1.call-start = ((), (), s32[]{:S(2)}) async-start(), calls=%async_computation.2 | async-start | bytes 17825792 | tf_op jit(solution)/shard_map/all_gather | solution.py:178
  9.7 361.9 %all-gather.3.cloned.1.call-start = ((), (), s32[]{:S(2)}) async-start(), calls=%async_computation.1 | async-start | bytes 35651584 | tf_op jit(solution)/shard_map/all_gather | solution.py:177
  11.6 6.0 %copy-start.10 = (bf16[512,1152]{1,0:T(8,128)(2,1)S(1)}, bf16[512,1152]{1,0:T(8,128)(2,1)}, u32[]{:S(2)}) copy-start(bf16[512,1152]{1,0:T(8,128)(2,1)} %param.33) | copy-start | bytes 3538948
  17.6 7.2 %copy-start.14 = (f32[512,2152]{0,1:T(8,128)}, f32[512,2152]{0,1:T(8,128)S(1)}, u32[]{:S(2)}) copy-start(f32[512,2152]{0,1:T(8,128)S(1)} %fusion.56) | copy-start | bytes 13221892
  30.7 70.2 %collective-permute-start.7 = (bf16[8,72,2152]{2,1,0:T(8,128)(2,1)}, bf16[8,72,2152]{2,1,0:T(8,128)(2,1)}, u32[]{:S(2)}, u32[]{:S(2)}) collective-permute-start(bf16[8,72,2152]{2,1,0:T(8,128)(2,1)} %fusion.16), channel_id=1, source_target_pairs={{0,2},{2,0},{4,6},{6,4},{8,10},{10,8},{12,14},{14,12},{16,18},{18,... | collective-permute-start | bytes 7437320 | tf_op jit(solution)/shard_map/ppermute | solution.py:147
  46.1 6.1 %copy-start.15 = (f32[512,2152]{0,1:T(8,128)S(1)}, f32[512,2152]{0,1:T(8,128)}, u32[]{:S(2)}) copy-start(f32[512,2152]{0,1:T(8,128)} %copy-done.14) | copy-start | bytes 13221892
  52.1 13.1 %copy-start.8 = (s32[16,16]{1,0:T(8,128)S(1)}, s32[16,16]{1,0:T(8,128)}, u32[]{:S(2)}) copy-start(s32[16,16]{1,0:T(8,128)} %param.26) | copy-start | bytes 3076
  52.1 13.5 %copy-start.2 = (s32[1,640]{1,0:T(1,128)S(1)}, s32[1,640]{1,0:T(1,128)}, u32[]{:S(2)}) copy-start(s32[1,640]{1,0:T(1,128)} %col_ref.1) | copy-start | bytes 7684
  52.1 62.4 %collective-permute-start.3 = (bf16[8,72,2152]{2,1,0:T(8,128)(2,1)}, bf16[8,72,2152]{2,1,0:T(8,128)(2,1)}, u32[]{:S(2)}, u32[]{:S(2)}) collective-permute-start(bf16[8,72,2152]{2,1,0:T(8,128)(2,1)} %fusion.15), channel_id=1, source_target_pairs={{0,2},{2,0},{4,6},{6,4},{8,10},{10,8},{12,14},{14,12},{16,18},{18,... | collective-permute-start | bytes 7437320 | tf_op jit(solution)/shard_map/ppermute | solution.py:147
  60.0 30.0 %collective-permute-start = (bf16[512,1152]{1,0:T(8,128)(2,1)}, bf16[512,1152]{1,0:T(8,128)(2,1)}, u32[]{:S(2)}, u32[]{:S(2)}) collective-permute-start(bf16[512,1152]{1,0:T(8,128)(2,1)} %get-tuple-element.17), channel_id=1, source_target_pairs={{0,1},{1,0},{2,3},{3,2},{4,5},{5,4},{6,7},{7,6},{8,9},{9,8},{10,11... | collective-permute-start | bytes 3538952 | tf_op jit(solution)/shard_map/ppermute | solution.py:115
  65.3 199.4 %collective-permute-start.2 = (bf16[128,4096]{1,0:T(8,128)(2,1)}, bf16[128,4096]{1,0:T(8,128)(2,1)}, u32[]{:S(2)}, u32[]{:S(2)}) collective-permute-start(bf16[128,4096]{1,0:T(8,128)(2,1)} %slice.71), channel_id=1, source_target_pairs={{0,1},{1,0},{2,3},{3,2},{4,5},{5,4},{6,7},{7,6},{8,9},{9,8},{10,11... | collective-permute-start | bytes 3145736 | tf_op jit(solution)/shard_map/ppermute | solution.py:115
  65.9 24.2 %copy-start.5 = (f32[512,1152]{1,0:T(8,128)S(1)}, f32[512,1152]{1,0:T(8,128)}, u32[]{:S(2)}) copy-start(f32[512,1152]{1,0:T(8,128)} %get-tuple-element.18) | copy-start | bytes 7077892
  94.0 20.6 %slice-start.2 = ((s8[10027008]{0:T(1024)(128)(4,1)}), s8[1638400]{0:T(1024)(128)(4,1)S(1)}, s32[]{:S(2)}) async-start(s8[10027008]{0:T(1024)(128)(4,1)} %bitcast.162), calls=%async_computation.5 | async-start | bytes 3276800
  94.0 50.2 %all-to-all-start = ((bf16[16,32,1152]{2,1,0:T(8,128)(2,1)}), bf16[16,32,1152]{2,1,0:T(8,128)(2,1)}, u32[]{:S(2)}, u32[]{:S(2)}) async-start(bf16[16,32,1152]{2,1,0:T(8,128)(2,1)} %bitcast.169), calls=%async_computation | async-start | bytes 2359296 | tf_op jit(solution)/shard_map/all_to_all | solution.py:203
  100.9 13.6 %slice-start.3 = ((s8[10027008]{0:T(1024)(128)(4,1)}), s8[4194304]{0:T(1024)(128)(4,1)S(1)}, s32[]{:S(2)}) async-start(s8[10027008]{0:T(1024)(128)(4,1)} %bitcast.162), calls=%async_computation.6 | async-start | bytes 8388608
  100.9 13.6 %slice-start.4 = ((s8[10027008]{0:T(1024)(128)(4,1)}), s8[4194304]{0:T(1024)(128)(4,1)S(1)}, s32[]{:S(2)}) async-start(s8[10027008]{0:T(1024)(128)(4,1)} %bitcast.162), calls=%async_computation.7 | async-start | bytes 8388608
  112.6 46.0 %collective-permute-start.8 = (bf16[4,72,2152]{2,1,0:T(8,128)(2,1)}, bf16[4,72,2152]{2,1,0:T(8,128)(2,1)}, u32[]{:S(2)}, u32[]{:S(2)}) collective-permute-start(bf16[4,72,2152]{2,1,0:T(8,128)(2,1)} %fusion.23), channel_id=1, source_target_pairs={{0,4},{2,6},{4,0},{6,2},{8,12},{10,14},{12,8},{14,10},{16,20},{18,... | collective-permute-start | bytes 3718664 | tf_op jit(solution)/shard_map/ppermute | solution.py:147
  116.9 2.3 copy-start.3
  120.5 62.9 %collective-permute-start.4 = (bf16[4,72,2152]{2,1,0:T(8,128)(2,1)}, bf16[4,72,2152]{2,1,0:T(8,128)(2,1)}, u32[]{:S(2)}, u32[]{:S(2)}) collective-permute-start(bf16[4,72,2152]{2,1,0:T(8,128)(2,1)} %fusion.22), channel_id=1, source_target_pairs={{0,4},{2,6},{4,0},{6,2},{8,12},{10,14},{12,8},{14,10},{16,20},{18,... | collective-permute-start | bytes 3718664 | tf_op jit(solution)/shard_map/ppermute | solution.py:147
  146.3 37.0 %slice-start = ((s8[5013504]{0:T(1024)(128)(4,1)}), s8[819200]{0:T(1024)(128)(4,1)S(1)}, s32[]{:S(2)}) async-start(s8[5013504]{0:T(1024)(128)(4,1)} %bitcast.158), calls=%async_computation.3 | async-start | bytes 1638400
  147.8 35.6 %slice-start.1 = ((s8[5013504]{0:T(1024)(128)(4,1)}), s8[4194304]{0:T(1024)(128)(4,1)S(1)}, s32[]{:S(2)}) async-start(s8[5013504]{0:T(1024)(128)(4,1)} %bitcast.158), calls=%async_computation.4 | async-start | bytes 8388608
  157.1 107.1 %collective-permute-start.1 = (bf16[512,4096]{1,0:T(8,128)(2,1)S(1)}, bf16[512,4096]{1,0:T(8,128)(2,1)S(1)}, u32[]{:S(2)}, u32[]{:S(2)}) collective-permute-start(bf16[512,4096]{1,0:T(8,128)(2,1)S(1)} %fusion.4), channel_id=1, source_target_pairs={{0,1},{1,0},{2,3},{3,2},{4,5},{5,4},{6,7},{7,6},{8,9},{9,8},{10,11... | collective-permute-start | bytes 12582920 | tf_op jit(solution)/shard_map/ppermute | solution.py:115
  161.9 41.5 %collective-permute-start.9 = (bf16[2,72,2152]{2,1,0:T(8,128)(2,1)S(1)}, bf16[2,72,2152]{2,1,0:T(8,128)(2,1)S(1)}, u32[]{:S(2)}, u32[]{:S(2)}) collective-permute-start(bf16[2,72,2152]{2,1,0:T(8,128)(2,1)S(1)} %fusion.30), channel_id=1, source_target_pairs={{0,8},{2,10},{4,12},{6,14},{8,0},{10,2},{12,4},{14,6},{16,24},{18,... | collective-permute-start | bytes 1859336 | tf_op jit(solution)/shard_map/ppermute | solution.py:147
  185.2 51.1 %collective-permute-start.5 = (bf16[2,72,2152]{2,1,0:T(8,128)(2,1)S(1)}, bf16[2,72,2152]{2,1,0:T(8,128)(2,1)S(1)}, u32[]{:S(2)}, u32[]{:S(2)}) collective-permute-start(bf16[2,72,2152]{2,1,0:T(8,128)(2,1)S(1)} %fusion.29), channel_id=1, source_target_pairs={{0,8},{2,10},{4,12},{6,14},{8,0},{10,2},{12,4},{14,6},{16,24},{18,... | collective-permute-start | bytes 1859336 | tf_op jit(solution)/shard_map/ppermute | solution.py:147
  203.6 39.6 %collective-permute-start.10 = (bf16[1,72,2152]{2,1,0:T(8,128)(2,1)S(1)}, bf16[1,72,2152]{2,1,0:T(8,128)(2,1)S(1)}, u32[]{:S(2)}, u32[]{:S(2)}) collective-permute-start(bf16[1,72,2152]{2,1,0:T(8,128)(2,1)S(1)} %fusion.35), channel_id=1, source_target_pairs={{0,16},{2,18},{4,20},{6,22},{8,24},{10,26},{12,28},{14,30},{16,0},... | collective-permute-start | bytes 929672 | tf_op jit(solution)/shard_map/ppermute | solution.py:147
  236.6 26.7 %collective-permute-start.6 = (bf16[1,72,2152]{2,1,0:T(8,128)(2,1)S(1)}, bf16[1,72,2152]{2,1,0:T(8,128)(2,1)S(1)}, u32[]{:S(2)}, u32[]{:S(2)}) collective-permute-start(bf16[1,72,2152]{2,1,0:T(8,128)(2,1)S(1)} %fusion.34), channel_id=1, source_target_pairs={{0,16},{2,18},{4,20},{6,22},{8,24},{10,26},{12,28},{14,30},{16,0},... | collective-permute-start | bytes 929672 | tf_op jit(solution)/shard_map/ppermute | solution.py:147
  266.0 4.6 %copy-start.6 = (f32[8192]{0:T(1024)S(1)}, f32[8192]{0:T(1024)}, u32[]{:S(2)}) copy-start(f32[8192]{0:T(1024)} %param.29) | copy-start | bytes 98308
  371.6 26.6 %copy-start = (f32[640,128]{1,0:T(8,128)S(1)}, f32[640,128]{1,0:T(8,128)}, u32[]{:S(2)}) copy-start(f32[640,128]{1,0:T(8,128)} %get-tuple-element.20.sin_ref) | copy-start | bytes 983044
  371.6 26.6 %copy-start.1 = (f32[640,1]{1,0:T(8,128)S(1)}, f32[640,1]{1,0:T(8,128)}, u32[]{:S(2)}) copy-start(f32[640,1]{1,0:T(8,128)} %broadcast_in_dim.76.inv_ref) | copy-start | bytes 7684
  (3 other events, 5.7 us)
Sparse Core Ops, SparseCore 0:
  10.2 152.4 all-gather.4
  164.2 207.2 all-gather.2
